TPU v7x, 256 devices: a whole 4x4x8 slice. The times are simulated.
256 devices in a mesh: dp: 128 (over z, x, y), pair: 2 (over core).
Axes of the slice: x: 4, y: 4, z: 8, core: 2. Of those that a mesh axis runs over, the one named last changes fastest.
Arguments:
- embeddings: float32 [65536, 1024], P(('dp', 'pair')), may hold values from -140 to 140
- block_ids: int32 [128, 2, 512], replicated, may hold values from 0 to 65536, as said below
- block_counts: int32 [128], replicated, may hold values from 0 to 2, as said below
Outputs:
- max_similarity: float32 [65536], P(('dp', 'pair'))
Inputs may be any that keep to these rules, and one draw needn't show every extreme that they name: `block_ids`: every document stands in exactly one live slot of one cluster; slots past a cluster's block_counts and the tail of its last block hold 65536; each device gives exactly 4 documents to clusters 2 i and 2 i + 1 together, and at most 4 to one cluster; some cluster takes 4 documents from every device and fills its 2 blocks. `block_counts`: the number of blocks that a cluster's documents fill.
All inputs are finite; a program needn't handle non-finite values.
Results may differ from a plain program's by a relative error of at most 0.0018.
Values may be sent and summed in bfloat16 or wider, within the bound.
No kernel may reach another device: no remote copies, remote signals or barrier semaphores. Data moves between devices by JAX's collectives and lax.ppermute only.
A program may use at most 64 MiB of HBM per device.

v0:
```python
from functools import partial

import jax
import jax.numpy as jnp
from jax import lax
from jax.sharding import PartitionSpec as P


def keep_same(best_sim):
    return best_sim


def strip_scores(members, live_slots, block_rows, row_block, best_sim):
    start_row = row_block * block_rows
    rows_first = members[start_row : start_row + block_rows]
    columns = members[start_row:]
    live_first = live_slots[start_row : start_row + block_rows]
    live_columns = live_slots[start_row:]
    scores = jnp.dot(rows_first, columns.T, preferred_element_type=jnp.float32)
    same_cell = jnp.arange(block_rows)[:, None] == jnp.arange(columns.shape[0])[None, :]
    row_best = jnp.max(jnp.where(live_columns[None, :] & ~same_cell, scores, -1.0), axis=1)
    col_best = jnp.max(jnp.where(live_first[:, None] & ~same_cell, scores, -1.0), axis=0)
    best_sim = best_sim.at[start_row:].set(jnp.maximum(best_sim[start_row:], col_best))
    return best_sim.at[start_row : start_row + block_rows].set(
        jnp.maximum(best_sim[start_row : start_row + block_rows], row_best)
    )


def body(embeddings, block_ids, block_counts):
    doc_rows, feature = embeddings.shape
    chip_count = lax.axis_size("dp")
    my_chip = lax.axis_index("dp")
    my_core = lax.axis_index("pair")
    cluster_total, max_blocks, block_rows = block_ids.shape
    slot_total = max_blocks * block_rows
    doc_total = doc_rows * 2 * chip_count
    capacity = 2 * doc_rows // chip_count
    id_table = block_ids.reshape(cluster_total, slot_total)
    slot_index = jnp.arange(slot_total, dtype=jnp.int32)
    live_table = (slot_index[None, :] // block_rows < block_counts[:, None]) & (
        id_table < doc_total
    )
    square = jnp.sum(embeddings * embeddings, axis=1, keepdims=True)
    normed = (embeddings * lax.rsqrt(square + 1e-06)).astype(jnp.bfloat16)
    group_size = 1
    first_doc = (my_chip * 2 + my_core) * doc_rows
    group_span = group_size * doc_rows
    width_cap = group_size * capacity
    mine_slots = live_table & (id_table >= first_doc) & (id_table < first_doc + group_span)
    block_index = jnp.arange(block_rows, dtype=jnp.int32)
    strict_upper = (block_index[:, None] < block_index[None, :]).astype(jnp.bfloat16)
    mine_blocks = mine_slots.reshape(cluster_total * max_blocks, block_rows).astype(jnp.bfloat16)
    within_rank = jnp.dot(mine_blocks, strict_upper, preferred_element_type=jnp.float32).astype(
        jnp.int32
    )
    block_total = jnp.sum(
        mine_slots.reshape(cluster_total, max_blocks, block_rows).astype(jnp.int32), axis=2
    )
    block_before = jnp.cumsum(block_total, axis=1) - block_total
    send_rank = (
        within_rank.reshape(cluster_total, max_blocks, block_rows) + block_before[:, :, None]
    ).reshape(cluster_total, slot_total)
    rank_slot = jnp.arange(width_cap, dtype=jnp.int32)
    chosen = mine_slots[:, None, :] & (send_rank[:, None, :] == rank_slot[None, :, None])
    local_offset = (id_table - first_doc)[:, None, :]
    local_at = jnp.sum(jnp.where(chosen, local_offset, 0), axis=2) + jnp.where(
        jnp.any(chosen, axis=2), 0, group_span
    )
    doc_index = jnp.arange(group_span, dtype=jnp.int32)
    pick_docs = local_at.reshape(-1)[:, None] == doc_index[None, :]
    packed = jnp.dot(
        pick_docs.astype(jnp.bfloat16), normed, preferred_element_type=jnp.float32
    ).astype(jnp.bfloat16)
    packed = packed.reshape(cluster_total, width_cap, feature)
    received = lax.all_to_all(packed, "dp", split_axis=0, concat_axis=0, tiled=True)
    own_ids = lax.dynamic_index_in_dim(id_table, my_chip, 0, keepdims=False)
    own_live = lax.dynamic_index_in_dim(live_table, my_chip, 0, keepdims=False)
    live_blocks = lax.dynamic_index_in_dim(block_counts, my_chip, 0, keepdims=False)
    group_total = 2 * chip_count // group_size
    src_group = jnp.where(own_live, own_ids // group_span, group_total)
    earlier_same = (
        (src_group[:, None] == src_group[None, :])
        & own_live[None, :]
        & (slot_index[:, None] > slot_index[None, :])
    )
    own_rank = jnp.sum(earlier_same.astype(jnp.int32), axis=1)
    gathered = lax.all_gather(received, "pair", axis=0, tiled=True)
    row_pool = gathered.reshape(2 * chip_count * capacity, feature)
    dest_chip = src_group // 2
    source_core = src_group % 2
    pool_row = (source_core * chip_count + dest_chip) * capacity + own_rank
    accept_slot = own_live & (source_core == my_core)
    pool_row = jnp.where(own_live, pool_row, row_pool.shape[0])
    pool_index = jnp.arange(row_pool.shape[0], dtype=jnp.int32)
    pick_rows = (pool_row[:, None] == pool_index[None, :]).astype(jnp.bfloat16)
    members = jnp.dot(pick_rows, row_pool, preferred_element_type=jnp.float32).astype(jnp.bfloat16)
    best_sim = jnp.full((slot_total,), -1.0, jnp.float32)
    for row_block in range(max_blocks):
        taken = (row_block % 2 == my_core) & (row_block < live_blocks)
        best_sim = lax.cond(
            taken,
            partial(strip_scores, members, own_live, block_rows, row_block),
            keep_same,
            best_sim,
        )
    best_sim = lax.pmax(best_sim, "pair")
    target_slot = jnp.where(accept_slot, dest_chip * width_cap + own_rank, chip_count * width_cap)
    buffer_index = jnp.arange(chip_count * width_cap, dtype=jnp.int32)
    lands = target_slot[None, :] == buffer_index[:, None]
    back_buffer = jnp.max(jnp.where(lands, best_sim[None, :], -1.0), axis=1)
    returned = lax.all_to_all(
        back_buffer.reshape(chip_count, width_cap), "dp", split_axis=0, concat_axis=0, tiled=True
    )
    result = jnp.max(jnp.where(pick_docs, returned.reshape(-1)[:, None], -1.0), axis=0)
    return result


def solution(mesh):
    in_specs = (P(("dp", "pair"), None), P(), P())
    out_specs = P(("dp", "pair"))
    return jax.shard_map(body, mesh=mesh, in_specs=in_specs, out_specs=out_specs, check_vma=False)
```

profile of v0, /device:TPU:1, one launch (start us, length us, event | category | flops | bytes accessed | tf_op | source)
XLA Modules:
  0.0 124.0 jit_solution(2684171854075505043)
XLA Ops:
  6.6 1.4 %multiply_reduce_fusion = f32[256]{0:T(256)S(1)} fusion(f32[256,1024]{1,0:T(8,128)} %param.17), kind=kLoop, calls=%fused_computation.37 | loop fusion | flops 524032 | bytes 1049600 | tf_op jit(solution)/shard_map/reduce_sum | solution.py:43
  8.0 0.8 lt.113
  9.1 0.4 lt.112
  9.6 3.7 %fusion.17 = (s32[128,2]{1,0:T(8,128)S(1)}, pred[128,2,512]{2,1,0:T(4,128)(4,1)S(1)}, pred[128,2,512]{2,1,0:T(4,128)(4,1)S(1)}, pred[128,2,512]{2,1,0:T(4,128)(4,1)S(1)}) fusion(s32[2,512]{1,0:T(2,128)S(1)} %and_select_fusion.4, s32[128]{0:T(128)S(1)} %copy-done.2, s32[128,2,512]{2,1,0:T(2,128)S(1)} %copy-done.1, s32[]{:T(128)S(6)} %mul.39, s32[]{:T(128)S(6)} %add.116), kind=kLoop, calls=%fused_computation.43 | loop fusion | flops 1179392 | bytes 923144 | tf_op jit(solution)/shard_map/reduce_sum | solution.py:56
  13.6 0.3 lt.119
  14.5 0.3 lt.122
  14.8 0.4 convolution_convert_fusion.1
  15.8 0.4 fusion.14
  16.2 0.5 select_reduce_fusion.5
  16.9 0.5 convolution_convert_fusion
  17.4 0.4 reshape.353
  17.9 44.8 %all_to_all.14 = bf16[128,4,1024]{2,1,0:T(4,128)(2,1)} all-to-all(bf16[128,4,1024]{2,1,0:T(4,128)(2,1)S(1)} %reshape.353), channel_id=1, replica_groups=mesh['dp'=128,'pair'=2] {'dp'}, dimensions={0} | all-to-all | bytes 2097152 | tf_op jit(solution)/shard_map/all_to_all | solution.py:75
  62.8 0.6 dynamic_slice.14
  64.8 0.6 convert_reduce_fusion
  65.5 10.3 %all-gather.2.cloned.1.call-done = bf16[256,4,1024]{2,1,0:T(4,128)(2,1)} async-done(((bf16[128,4,1024]{2,1,0:T(4,128)(2,1)}), bf16[256,4,1024]{2,1,0:T(4,128)(2,1)}) %all-gather.2.cloned.1.call-update) | async-done | bytes 2097168 | tf_op jit(solution)/shard_map/all_gather | solution.py:87
  75.7 2.5 %reshape.354 = bf16[1024,1024]{1,0:T(8,128)(2,1)S(1)} reshape(bf16[256,4,1024]{2,1,0:T(4,128)(2,1)} %all-gather.2.cloned.1.call-done) | data formatting | bytes 4194304 | tf_op jit(solution)/shard_map/reshape | solution.py:88
  78.3 3.7 %fusion.15 = bf16[1024,1024]{1,0:T(8,128)(2,1)} fusion(bf16[1024,1024]{1,0:T(8,128)(2,1)S(1)} %reshape.354, s32[1024]{0:T(1024)S(1)} %fusion.30), kind=kOutput, calls=%fused_computation.33 | convolution fusion | flops 2149580800 | bytes 4198400 | tf_op jit(solution)/shard_map/dot_general | solution.py:96
  82.0 0.6 conditional.2
  82.0 0.6 broadcast_in_dim.55
  82.6 7.8 %pmax.7 = f32[1024]{0:T(1024)S(1)} all-reduce(f32[1024]{0:T(1024)} %get-tuple-element.96), channel_id=1, replica_groups=mesh['dp'=128,'pair'=2] {'pair'}, use_global_device_ids=true, to_apply=%region_14.15 | all-reduce | flops 1024 | bytes 8192 | tf_op jit(solution)/shard_map/pmax | solution.py:106
  90.8 24.1 %all_to_all.15 = f32[128,1,4]{2,1,0:T(1,128)S(1)} all-to-all(f32[128,1,4]{2,1,0:T(1,128)S(1)} %bitcast.21), channel_id=1, replica_groups=mesh['dp'=128,'pair'=2] {'dp'}, dimensions={0} | all-to-all | bytes 4096 | tf_op jit(solution)/shard_map/all_to_all | solution.py:111
  114.9 0.5 broadcast.371
  115.4 0.8 reduce.13
  116.4 0.8 select_reduce_fusion.6
  (35 shorter events, 2.7 us)
Async XLA Ops:
  6.5 2.9 %copy-start.1 = (s32[128,2,512]{2,1,0:T(2,128)S(1)}, s32[128,2,512]{2,1,0:T(2,128)}, u32[]{:S(2)}) copy-start(s32[128,2,512]{2,1,0:T(2,128)} %param.18) | copy-start | bytes 1572868
  6.5 69.2 %all-gather.2.cloned.1.call-start = ((), (), s32[]{:S(2)}) async-start(), calls=%async_computation.2 | async-start | bytes 3145728 | tf_op jit(solution)/shard_map/all_gather | solution.py:87
  8.0 1.6 %copy-start.2 = (s32[128]{0:T(128)S(1)}, s32[128]{0:T(128)}, u32[]{:S(2)}) copy-start(s32[128]{0:T(128)} %param.19) | copy-start | bytes 1540
  15.6 1.3 %copy-start = (f32[256,1024]{1,0:T(8,128)S(1)}, f32[256,1024]{1,0:T(8,128)}, u32[]{:S(2)}) copy-start(f32[256,1024]{1,0:T(8,128)} %param.17) | copy-start | bytes 3145732
Sparse Core Ops, SparseCore 0:
  62.9 12.8 all-gather.1
where the time goes:
time: 124 us
  blocking collectives  76.8 us (62%)
  between operations  15 us (12%)
  waiting for transfers between devices  10.3 us (8%)
  other arithmetic  9.27 us (7%)
  local copies, waits for them, and re-layouts  8.07 us (7%)
  matrix products  4.63 us (4%)
    all_to_all x1, blocking collectives, body(): lax.all_to_all(packed, 'dp', split_axis=0, concat_axis=0, tiled=True)  44.8 us
    all_to_all x1, blocking collectives, body(): lax.all_to_all(back_buffer.reshape(chip_count, width_cap), 'dp', split_ax...  24.1 us
    all_gather x1, waiting for transfers between devices, body(): gathered = lax.all_gather(received, 'pair', axis=0, tiled=True)  10.3 us
    pmax x1, blocking collectives, body(): best_sim = lax.pmax(best_sim, 'pair')  7.8 us
    reduce_sum x1, other arithmetic, body(): jnp.sum(mine_slots.reshape(cluster_total, max_blocks, block_rows).astype(...  3.73 us
    dot_general x1, matrix products, body(): jnp.dot(pick_rows, row_pool, preferred_element_type=jnp.float32)  3.73 us
    reshape x1, local copies, waits for them, and re-layouts, body(): row_pool = gathered.reshape(2 * chip_count * capacity, feature)  2.54 us
  transfers between devices with their start and end apart: 1, of which 1 were waited for; matrix products, arithmetic and copies ran while one was open for 1% of the time, Pallas kernels for 0%

commit v1 on v0

v1 whole, which is shorter than its diff:
```python
from functools import partial

import jax
import jax.numpy as jnp
from jax import lax
from jax.experimental import pallas as pl
from jax.experimental.pallas import tpu as pltpu
from jax.sharding import PartitionSpec as P

BF16 = jnp.bfloat16
F32 = jnp.float32
I32 = jnp.int32
VMEM_LIMIT = 48 * 1024 * 1024


def iota(shape, dim):
    return lax.broadcasted_iota(I32, shape, dim)


def pack_kernel(first_ref, emb_ref, ids_ref, counts_ref, packed_ref, doc_ref):
    doc_rows = emb_ref.shape[0]
    clusters, blocks, block_rows = ids_ref.shape
    doc_total = doc_rows * 2 * clusters
    first = first_ref[0]
    diagonal = iota((clusters, clusters), 0) == iota((clusters, clusters), 1)
    counts = jnp.sum(
        jnp.where(diagonal, jnp.broadcast_to(counts_ref[...], (clusters, clusters)), 0),
        axis=1,
        keepdims=True,
    )
    even = iota((clusters, 1), 0) % 2 == 0
    lift = jnp.where(even, doc_rows, 0)
    keys = []
    for block in range(blocks):
        ids = ids_ref[:, block, :]
        local = ids - first
        mine = (local >= 0) & (local < doc_rows) & (block < counts) & (ids < doc_total)
        keys.append(jnp.where(mine, local + lift, -1).astype(F32))
    lane = iota((clusters, 128), 1)
    even_wide = iota((clusters, 128), 0) % 2 == 0
    picked = jnp.zeros((clusters, 128), F32)
    for rank in range(4):
        best = jnp.maximum(
            jnp.max(keys[0], axis=1, keepdims=True), jnp.max(keys[1], axis=1, keepdims=True)
        )
        wide = jnp.broadcast_to(best, (clusters, 128))
        other = jnp.where(
            even_wide, pltpu.roll(wide, clusters - 1, 0), pltpu.roll(wide, 1, 0)
        )
        top_wide = jnp.maximum(wide, other)
        top = top_wide[:, :1]
        if rank < 3:
            keys = [jnp.where(key == top, -1.0, key) for key in keys]
        doc = jnp.where(top_wide >= doc_rows, top_wide - doc_rows, top_wide)
        picked = jnp.where(lane == rank, doc, picked)
    picked = picked.astype(BF16)
    pairs = clusters // 2
    take_pair = (iota((pairs, clusters), 1) == 2 * iota((pairs, clusters), 0)).astype(BF16)
    doc_ref[...] = jnp.dot(take_pair, picked, preferred_element_type=F32).astype(I32)
    rows = 4 * pairs
    row = iota((rows, clusters), 0)
    spread = (iota((rows, clusters), 1) == 2 * (row // 4)).astype(BF16)
    by_row = jnp.dot(spread, picked, preferred_element_type=F32)
    lane_row = iota((rows, 128), 1) == iota((rows, 128), 0) % 4
    doc_of_row = jnp.sum(jnp.where(lane_row, by_row, 0.0), axis=1, keepdims=True).astype(I32)
    pick = (doc_of_row == iota((rows, doc_rows), 1)).astype(BF16)
    emb = emb_ref[...]
    square = jnp.sum(emb * emb, axis=1, keepdims=True)
    normed = (emb * lax.rsqrt(square + 1e-06)).astype(BF16)
    packed_ref[...] = jnp.dot(pick, normed, preferred_element_type=F32).astype(BF16)


def pack(first, embeddings, block_ids, counts):
    doc_rows, feature = embeddings.shape
    clusters = block_ids.shape[0]
    return pl.pallas_call(
        pack_kernel,
        out_shape=(
            jax.ShapeDtypeStruct((2 * clusters, feature), BF16),
            jax.ShapeDtypeStruct((clusters // 2, 128), I32),
        ),
        in_specs=[
            pl.BlockSpec(memory_space=pltpu.SMEM),
            pl.BlockSpec(memory_space=pltpu.VMEM),
            pl.BlockSpec(memory_space=pltpu.VMEM),
            pl.BlockSpec(memory_space=pltpu.VMEM),
        ],
        out_specs=(
            pl.BlockSpec(memory_space=pltpu.VMEM),
            pl.BlockSpec(memory_space=pltpu.VMEM),
        ),
        compiler_params=pltpu.CompilerParams(vmem_limit_bytes=VMEM_LIMIT),
        name="pack",
    )(first, embeddings, block_ids, counts)


def source_of(chip_base, core, group):
    own = group // 128 == 0
    of_core = jnp.where(own, core, 1 - core)
    hop = jnp.where(of_core == 0, 4, 1)
    chip = jnp.where((group // 64) % 2 == 0, chip_base, chip_base ^ hop)
    return chip * 2 + of_core


def owner_chip(position):
    z, x, half = position // 8, (position // 2) % 4, position % 2
    return z * 16 + x * 4 + half * 2 + (z + x) % 2


def label_kernel(where_ref, ids_ref, counts_ref, row_ref, col_ref):
    _, blocks, block_rows = ids_ref.shape
    core, cluster, doc_rows = where_ref[0], where_ref[1], where_ref[2]
    count = counts_ref[cluster]
    group = iota((256, 1), 0)
    source = source_of(owner_chip(group % 64), core, group)
    hits = jnp.zeros((256, block_rows), F32)
    for block in range(blocks):
        ids = ids_ref[0, block : block + 1, :]
        slot_source = jnp.where(block < count, ids >> 8, -1)
        hits = hits + jnp.where(source == slot_source, 1.0, 0.0)
    tally = jnp.sum(hits, axis=1, keepdims=True)
    tally_wide = jnp.broadcast_to(tally, (256, 128)).astype(BF16)
    col_spread = (iota((1024, 256), 0) // 4 == iota((1024, 256), 1)).astype(BF16)
    by_row = jnp.dot(col_spread, tally_wide, preferred_element_type=F32)
    rank = (iota((1024, 128), 0) % 4).astype(F32)
    col = jnp.where(rank >= by_row, 1.0, 0.0)
    col_ref[...] = col
    row_ref[...] = jnp.transpose(col[:512])[:8]


def labels(where, block_ids, counts):
    clusters, blocks, block_rows = block_ids.shape
    return pl.pallas_call(
        label_kernel,
        out_shape=(
            jax.ShapeDtypeStruct((8, 512), F32),
            jax.ShapeDtypeStruct((1024, 128), F32),
        ),
        grid_spec=pltpu.PrefetchScalarGridSpec(
            num_scalar_prefetch=1,
            grid=(1,),
            in_specs=[
                pl.BlockSpec((1, blocks, block_rows), lambda i, where: (where[1], 0, 0)),
                pl.BlockSpec(memory_space=pltpu.SMEM),
            ],
            out_specs=(
                pl.BlockSpec((8, 512), lambda i, where: (0, 0)),
                pl.BlockSpec((1024, 128), lambda i, where: (0, 0)),
            ),
        ),
        compiler_params=pltpu.CompilerParams(vmem_limit_bytes=VMEM_LIMIT),
        name="labels",
    )(where, block_ids, counts)


def score_kernel(row_ref, col_ref, a_ref, b_ref, c_ref, d_ref, best_ref):
    own = jnp.concatenate([a_ref[...], b_ref[...]], axis=0)
    label = row_ref[0:1, :]
    top = jnp.full((1, 512), -1.0, F32)
    for part, ref in enumerate((a_ref, b_ref, c_ref, d_ref)):
        scores = lax.dot_general(
            ref[...], own, (((1,), (1,)), ((), ())), preferred_element_type=F32
        )
        same = col_ref[part * 256 : (part + 1) * 256, 0:1] == label
        if part < 2:
            same = same & (iota((256, 512), 0) + part * 256 != iota((256, 512), 1))
        top = jnp.maximum(top, jnp.max(jnp.where(same, scores, -1.0), axis=0, keepdims=True))
    slot, member = iota((128, 512), 0), iota((128, 512), 1)
    spread = jnp.where(member // 4 == slot, jnp.broadcast_to(top, (128, 512)), -1.0)
    for rank in range(4):
        best_ref[:, rank : rank + 1] = jnp.max(
            jnp.where(member % 4 == rank, spread, -1.0), axis=1, keepdims=True
        )


def score(row, col, a, b, c, d):
    return pl.pallas_call(
        score_kernel,
        out_shape=jax.ShapeDtypeStruct((128, 4), F32),
        in_specs=[pl.BlockSpec(memory_space=pltpu.VMEM)] * 6,
        out_specs=pl.BlockSpec(memory_space=pltpu.VMEM),
        compiler_params=pltpu.CompilerParams(vmem_limit_bytes=VMEM_LIMIT),
        name="score",
    )(row, col, a, b, c, d)


def unpack_kernel(doc_ref, back_ref, out_ref):
    pairs = doc_ref.shape[0]
    doc_rows = out_ref.shape[1]
    doc_lane = iota((pairs, doc_rows), 1)
    top = jnp.full((pairs, doc_rows), -1.0, F32)
    for rank in range(4):
        hit = doc_ref[:, rank : rank + 1] == doc_lane
        top = jnp.maximum(top, jnp.where(hit, back_ref[0:pairs, rank : rank + 1], -1.0))
    out_ref[...] = jnp.max(top, axis=0, keepdims=True)


def unpack(docs, back, doc_rows):
    return pl.pallas_call(
        unpack_kernel,
        out_shape=jax.ShapeDtypeStruct((1, doc_rows), F32),
        in_specs=[pl.BlockSpec(memory_space=pltpu.VMEM)] * 2,
        out_specs=pl.BlockSpec(memory_space=pltpu.VMEM),
        name="unpack",
    )(docs, back)


def chip_groups():
    owners = [z * 16 + x * 4 + y for z in range(8) for x in range(4) for y in range(4) if (z + x + y) % 2 == 0]
    direct, passing, back, forward, swap = [], [], [], [], []
    for core in range(2):
        hop = 4 if core == 0 else 1
        direct.append([chip * 2 + core for chip in owners])
        passing.append([(chip ^ hop) * 2 + core for chip in owners])
        back.append(direct[-1] + passing[-1])
        forward += list(zip(passing[-1], direct[-1]))
    for chip in range(128):
        swap += [(chip * 2, chip * 2 + 1), (chip * 2 + 1, chip * 2)]
    return direct + passing, back, forward, swap


def body(embeddings, block_ids, block_counts):
    doc_rows, feature = embeddings.shape
    my_chip = lax.axis_index("dp").astype(I32)
    my_core = lax.axis_index("pair").astype(I32)
    send_groups, back_groups, forward, swap = chip_groups()
    both = ("dp", "pair")
    z, x, y = my_chip // 16, (my_chip // 4) % 4, my_chip % 4
    position = z * 8 + x * 2 + y // 2
    first = ((my_chip * 2 + my_core) * doc_rows).reshape(1)
    packed, docs = pack(first, embeddings, block_ids, block_counts.reshape(1, -1))
    packed = packed.reshape(64, 4, feature)
    direct = lax.all_to_all(
        packed, both, split_axis=0, concat_axis=0, axis_index_groups=send_groups, tiled=True
    )
    direct = direct.reshape(256, feature)
    passed = lax.ppermute(direct, both, forward)
    direct_other = lax.ppermute(direct, both, swap)
    where = jnp.stack([my_core, 2 * position, jnp.full_like(my_core, doc_rows)])
    row, col = labels(where, block_ids, block_counts)
    passed_other = lax.ppermute(passed, both, swap)
    best = score(row, col, direct, passed, direct_other, passed_other)
    back = lax.all_to_all(
        best, both, split_axis=0, concat_axis=0, axis_index_groups=back_groups, tiled=True
    )
    return unpack(docs, back, doc_rows).reshape(doc_rows)


def solution(mesh):
    in_specs = (P(("dp", "pair"), None), P(), P())
    out_specs = P(("dp", "pair"))
    return jax.shard_map(body, mesh=mesh, in_specs=in_specs, out_specs=out_specs, check_vma=False)
```

time: 124 us -> 74.8 us (0.60)
  blocking collectives: 76.8 us -> 49.3 us
  between operations: 15 us -> 0.05 us
  starting transfers between devices: 0.01 us -> 9.49 us
  other arithmetic: 9.27 us -> 0.08 us
  Pallas kernels: 0 us -> 6.46 us
  waiting for transfers between devices: 10.3 us -> 5.28 us
  matrix products: 4.63 us -> 0 us
  local copies, waits for them, and re-layouts: 8.07 us -> 3.84 us
    all_to_all x2, blocking collectives: 69 us -> 49.3 us  [the longest x1 31.6 us: body(): lax.all_to_all(packed, both, split_axis=0, concat_axis=0, axis_index_grou...]
    all_gather x1 -> x0, waiting for transfers between devices: 10.3 us -> none  [body(): gathered = lax.all_gather(received, 'pair', axis=0, tiled=True)]
    ppermute x0 -> x3, starting transfers between devices: none -> 9.49 us  [the longest x1 4.42 us: body(): passed_other = lax.ppermute(passed, both, swap)]
    pmax x1 -> x0, blocking collectives: 7.8 us -> none  [body(): best_sim = lax.pmax(best_sim, 'pair')]
    pallas_call x0 -> x4, Pallas kernels: none -> 6.46 us  [the longest x1 1.73 us: pack(): pl.pallas_call(pack_kernel, out_shape=(jax.ShapeDtypeStruct((2 * clusters...]
    reduce_sum x4 -> x0, other arithmetic: 6.28 us -> none  [the longest x1 3.73 us: body(): jnp.sum(mine_slots.reshape(cluster_total, max_blocks, block_rows).astype(...]
    ppermute x0 -> x3, waiting for transfers between devices: none -> 5.28 us  [the longest x1 5.27 us: body(): passed = lax.ppermute(direct, both, forward)]
    dot_general x3 -> x0, matrix products: 4.63 us -> none  [the longest x1 3.73 us: body(): jnp.dot(pick_rows, row_pool, preferred_element_type=jnp.float32)]
  transfers between devices with their start and end apart: 1 -> 3, of which waited for: 1 -> 1; matrix products, arithmetic and copies ran while one was open for 1% -> 0% of each run, Pallas kernels for 0% -> 2%
where the time goes in v1:
time: 74.8 us; the launch traced here: 74.5 us
  blocking collectives  49.3 us (66%)
  starting transfers between devices  9.49 us (13%)
  Pallas kernels  6.46 us (9%)
  waiting for transfers between devices  5.28 us (7%)
  local copies, waits for them, and re-layouts  3.84 us (5%)
    all_to_all x1, blocking collectives, body(): lax.all_to_all(packed, both, split_axis=0, concat_axis=0, axis_index_grou...  31.6 us
    all_to_all x1, blocking collectives, body(): lax.all_to_all(best, both, split_axis=0, concat_axis=0, axis_index_groups...  17.7 us
    ppermute x1, waiting for transfers between devices, body(): passed = lax.ppermute(direct, both, forward)  5.27 us
    ppermute x1, starting transfers between devices, body(): passed_other = lax.ppermute(passed, both, swap)  4.42 us
    ppermute x1, starting transfers between devices, body(): direct_other = lax.ppermute(direct, both, swap)  3.65 us
    unnamed x10, local copies, waits for them, and re-layouts  3.52 us
    pallas_call x1, Pallas kernels, pack(): pl.pallas_call(pack_kernel, out_shape=(jax.ShapeDtypeStruct((2 * clusters...  1.73 us
    pallas_call x1, Pallas kernels, labels(): pl.pallas_call(label_kernel, out_shape=(jax.ShapeDtypeStruct((8, 512), F3...  1.7 us
  transfers between devices with their start and end apart: 3, of which 1 were waited for; matrix products, arithmetic and copies ran while one was open for 0% of the time, Pallas kernels for 2%

profile of v1, /device:TPU:1, one launch (start us, length us, event | category | flops | bytes accessed | tf_op | source)
XLA Modules:
  0.0 74.5 jit_solution(11942127614167218618)
XLA Ops:
  0.0 0.7 copy-done.4
  0.7 0.0 copy-start
  0.7 1.0 %copy-done = s32[128,2,512]{2,1,0:T(2,128)S(1)} copy-done((s32[128,2,512]{2,1,0:T(2,128)S(1)}, s32[128,2,512]{2,1,0:T(2,128)}, u32[]{:S(2)}) %copy-start) | copy-done | bytes 524312
  1.7 0.0 copy-start.2
  1.7 1.2 %copy-done.2 = f32[256,1024]{1,0:T(8,128)S(1)} copy-done((f32[256,1024]{1,0:T(8,128)S(1)}, f32[256,1024]{1,0:T(8,128)}, u32[]{:S(2)}) %copy-start.2) | copy-done | bytes 1048600
  2.9 1.7 %pack.1 = (bf16[256,1024]{1,0:T(8,128)(2,1)S(1)}, s32[64,128]{1,0:T(8,128)S(1)}) custom-call(s32[1]{0:T(128)} %bitcast.first_ref, f32[256,1024]{1,0:T(8,128)S(1)} %copy-done.2, s32[128,2,512]{2,1,0:T(2,128)S(1)} %copy-done, s32[1,128]{1,0:T(1,128)S(1)} %bitcast.10), custom_call_target="tpu_custom_call" | custom-call | tf_op jit(solution)/shard_map/pack/pallas_call | solution.py:76
  4.7 0.0 copy-start.3
  4.7 0.6 copy-done.3
  5.3 0.2 reshape.19
  5.5 31.6 %all_to_all.16 = bf16[64,4,1024]{2,1,0:T(4,128)(2,1)S(1)} all-to-all(bf16[64,4,1024]{2,1,0:T(4,128)(2,1)S(1)} %reshape.19), channel_id=1, replica_groups={{0,4,10,14,16,20,26,30,34,38,40,44,50,54,56,60,64,68,74,78,80,84,90,94,..., dimensions={0} | all-to-all | bytes 1048576 | tf_op jit(solution)/shard_map/all_to_all | solution.py:233
  37.1 0.0 copy-start.1
  37.1 0.1 reshape.20.a_ref
  37.2 1.4 %collective-permute-start = (bf16[256,1024]{1,0:T(8,128)(2,1)S(1)}, bf16[256,1024]{1,0:T(8,128)(2,1)S(1)}, u32[]{:S(2)}, u32[]{:S(2)}) collective-permute-start(bf16[256,1024]{1,0:T(8,128)(2,1)S(1)} %reshape.20.a_ref), channel_id=1, source_target_pairs={{8,0},{12,4},{2,10},{6,14},{24,16},{28,20},{18,26},{22,30},{42,34}... | collective-permute-start | bytes 1572872 | tf_op jit(solution)/shard_map/ppermute | solution.py:237
  38.6 3.6 %collective-permute-start.1 = (bf16[256,1024]{1,0:T(8,128)(2,1)S(1)}, bf16[256,1024]{1,0:T(8,128)(2,1)S(1)}, u32[]{:S(2)}, u32[]{:S(2)}) collective-permute-start(bf16[256,1024]{1,0:T(8,128)(2,1)S(1)} %reshape.20.a_ref), channel_id=1, source_target_pairs={{0,1},{1,0},{2,3},{3,2},{4,5},{5,4},{6,7},{7,6},{8,9},{9,8},{10,11... | collective-permute-start | bytes 1572872 | tf_op jit(solution)/shard_map/ppermute | solution.py:238
  42.3 5.3 %collective-permute-done.b_ref = bf16[256,1024]{1,0:T(8,128)(2,1)S(1)} collective-permute-done((bf16[256,1024]{1,0:T(8,128)(2,1)S(1)}, bf16[256,1024]{1,0:T(8,128)(2,1)S(1)}, u32[]{:S(2)}, u32[]{:S(2)}) %collective-permute-start) | collective-permute-done | bytes 524320 | tf_op jit(solution)/shard_map/ppermute | solution.py:237
  47.6 4.4 %collective-permute-start.2 = (bf16[256,1024]{1,0:T(8,128)(2,1)S(1)}, bf16[256,1024]{1,0:T(8,128)(2,1)S(1)}, u32[]{:S(2)}, u32[]{:S(2)}) collective-permute-start(bf16[256,1024]{1,0:T(8,128)(2,1)S(1)} %collective-permute-done.b_ref), channel_id=1, source_target_pairs={{0,1},{1,0},{2,3},{3,2},{4,5},{5,4},{6,7},{7,6},{8,9},{9,8},{10,11... | collective-permute-start | bytes 1572872 | tf_op jit(solution)/shard_map/ppermute | solution.py:241
  52.0 0.1 pad_add_fusion.where_ref
  52.0 0.0 copy-done.1
  52.0 1.7 %labels.1 = (f32[8,512]{1,0:T(8,128)S(1)}, f32[1024,128]{1,0:T(8,128)S(1)}) custom-call(s32[3]{0:T(128)S(1)} %pad_add_fusion.where_ref, s32[128,2,512]{2,1,0:T(2,128)S(1)} %copy-done.1, s32[128]{0:T(128)S(1)} %copy-done.4), custom_call_target="tpu_custom_call" | custom-call | tf_op jit(solution)/shard_map/labels/pallas_call | solution.py:133
  53.8 0.0 collective-permute-done.1.c_ref
  53.8 0.0 collective-permute-done.2.d_ref
  53.8 1.5 %score.1 = f32[128,4]{1,0:T(8,128)S(1)} custom-call(f32[8,512]{1,0:T(8,128)S(1)} %get-tuple-element.10.row_ref, f32[1024,128]{1,0:T(8,128)S(1)} %get-tuple-element.11.col_ref, bf16[256,1024]{1,0:T(8,128)(2,1)S(1)} %reshape.20.a_ref, bf16[256,1024]{1,0:T(8,128)(2,1)S(1)} %collective-permute-done.b_ref, bf16[256,1024]{1,0:T(8,128)(2,1)S(1)} %collective-permute-done.1.c_ref, ...), custom_call_target="tpu_custom_call" | custom-call | tf_op jit(solution)/shard_map/score/pallas_call | solution.py:177
  55.2 17.7 %all_to_all.17 = f32[128,1,4]{2,1,0:T(1,128)} all-to-all(f32[128,1,4]{2,1,0:T(1,128)S(1)} %bitcast.9), channel_id=1, replica_groups={{0,4,10,14,16,20,26,30,34,38,40,44,50,54,56,60,64,68,74,78,80,84,90,94,..., dimensions={0} | all-to-all | bytes 4096 | tf_op jit(solution)/shard_map/all_to_all | solution.py:243
  72.9 1.6 %unpack.1 = f32[1,256]{1,0:T(1,128)} custom-call(s32[64,128]{1,0:T(8,128)} %copy-done.3, f32[128,4]{1,0:T(8,128)} %bitcast.11), custom_call_target="tpu_custom_call" | custom-call | tf_op jit(solution)/shard_map/unpack/pallas_call | solution.py:199
  (1 shorter events, 0.0 us)
Async XLA Ops:
  0.0 0.7 copy-start.4
  0.7 1.0 %copy-start = (s32[128,2,512]{2,1,0:T(2,128)S(1)}, s32[128,2,512]{2,1,0:T(2,128)}, u32[]{:S(2)}) copy-start(s32[128,2,512]{2,1,0:T(2,128)} %ids_ref.3) | copy-start | bytes 1572868
  1.7 1.2 %copy-start.2 = (f32[256,1024]{1,0:T(8,128)S(1)}, f32[256,1024]{1,0:T(8,128)}, u32[]{:S(2)}) copy-start(f32[256,1024]{1,0:T(8,128)} %emb_ref.1) | copy-start | bytes 3145732
  4.7 0.6 copy-start.3
  37.1 15.0 %copy-start.1 = (s32[128,2,512]{2,1,0:T(2,128)S(1)}, s32[128,2,512]{2,1,0:T(2,128)}, u32[]{:S(2)}) copy-start(s32[128,2,512]{2,1,0:T(2,128)} %ids_ref.3) | copy-start | bytes 1572868
  37.2 10.4 %collective-permute-start = (bf16[256,1024]{1,0:T(8,128)(2,1)S(1)}, bf16[256,1024]{1,0:T(8,128)(2,1)S(1)}, u32[]{:S(2)}, u32[]{:S(2)}) collective-permute-start(bf16[256,1024]{1,0:T(8,128)(2,1)S(1)} %reshape.20.a_ref), channel_id=1, source_target_pairs={{8,0},{12,4},{2,10},{6,14},{24,16},{28,20},{18,26},{22,30},{42,34}... | collective-permute-start | bytes 1572872 | tf_op jit(solution)/shard_map/ppermute | solution.py:237
  38.6 15.1 %collective-permute-start.1 = (bf16[256,1024]{1,0:T(8,128)(2,1)S(1)}, bf16[256,1024]{1,0:T(8,128)(2,1)S(1)}, u32[]{:S(2)}, u32[]{:S(2)}) collective-permute-start(bf16[256,1024]{1,0:T(8,128)(2,1)S(1)} %reshape.20.a_ref), channel_id=1, source_target_pairs={{0,1},{1,0},{2,3},{3,2},{4,5},{5,4},{6,7},{7,6},{8,9},{9,8},{10,11... | collective-permute-start | bytes 1572872 | tf_op jit(solution)/shard_map/ppermute | solution.py:238
  47.6 6.2 %collective-permute-start.2 = (bf16[256,1024]{1,0:T(8,128)(2,1)S(1)}, bf16[256,1024]{1,0:T(8,128)(2,1)S(1)}, u32[]{:S(2)}, u32[]{:S(2)}) collective-permute-start(bf16[256,1024]{1,0:T(8,128)(2,1)S(1)} %collective-permute-done.b_ref), channel_id=1, source_target_pairs={{0,1},{1,0},{2,3},{3,2},{4,5},{5,4},{6,7},{7,6},{8,9},{9,8},{10,11... | collective-permute-start | bytes 1572872 | tf_op jit(solution)/shard_map/ppermute | solution.py:241

commit v2 on v1

v2 whole, which is shorter than its diff:
```python
from functools import partial

import jax
import jax.numpy as jnp
from jax import lax
from jax.experimental import pallas as pl
from jax.experimental.pallas import tpu as pltpu
from jax.sharding import PartitionSpec as P

BF16 = jnp.bfloat16
F32 = jnp.float32
I32 = jnp.int32
MIB = 1024 * 1024
BOTH = ("dp", "pair")


def iota(shape, dim):
    return lax.broadcasted_iota(I32, shape, dim)


def in_vmem(count):
    return [pl.BlockSpec(memory_space=pltpu.VMEM)] * count


def my_place():
    return lax.axis_index("dp").astype(I32), lax.axis_index("pair").astype(I32)


def chip_parity(chip):
    return ((chip >> 4) + (chip >> 2) + chip) & 1


def chip_position(chip):
    return chip >> 1


def owner_chip(position):
    return 2 * position + (((position >> 3) + (position >> 1)) & 1)


def pack_kernel(
    emb_hbm, ids_hbm, counts_hbm, packed_ref, doc_ref, emb_ref, ids_ref, counts_ref, sems
):
    copies = [
        pltpu.make_async_copy(counts_hbm, counts_ref, sems.at[0]),
        pltpu.make_async_copy(ids_hbm, ids_ref, sems.at[1]),
        pltpu.make_async_copy(emb_hbm, emb_ref, sems.at[2]),
    ]
    for copy in copies:
        copy.start()
    doc_rows = emb_ref.shape[0]
    clusters, blocks, block_rows = ids_ref.shape
    doc_total = doc_rows * 2 * clusters
    chip, core = my_place()
    first = (chip * 2 + core) * doc_rows
    turned = (chip_parity(chip) == 1) & (chip >= clusters // 2)
    flip = jnp.where(turned, jnp.where(core == 0, 4, 1), 0)
    diagonal = iota((clusters, clusters), 0) == iota((clusters, clusters), 1)
    even = iota((clusters, 1), 0) % 2 == 0
    lift = jnp.where(even, doc_rows, 0)
    lane = iota((clusters, 128), 1)
    even_wide = iota((clusters, 128), 0) % 2 == 0
    copies[0].wait()
    counts = jnp.sum(
        jnp.where(diagonal, jnp.broadcast_to(counts_ref[...], (clusters, clusters)), 0),
        axis=1,
        keepdims=True,
    )
    copies[1].wait()
    keys = []
    for block in range(blocks):
        ids = ids_ref[:, block, :]
        local = ids - first
        mine = (local >= 0) & (local < doc_rows) & (block < counts) & (ids < doc_total)
        keys.append(jnp.where(mine, local + lift, -1).astype(F32))
    picked = jnp.zeros((clusters, 128), F32)
    for rank in range(4):
        best = jnp.max(jnp.maximum(keys[0], keys[1]), axis=1, keepdims=True)
        wide = jnp.broadcast_to(best, (clusters, 128))
        other = jnp.where(
            even_wide, pltpu.roll(wide, clusters - 1, 0), pltpu.roll(wide, 1, 0)
        )
        top_wide = jnp.maximum(wide, other)
        top = top_wide[:, :1]
        if rank < 3:
            keys = [jnp.where(key == top, -1.0, key) for key in keys]
        doc = jnp.where(top_wide >= doc_rows, top_wide - doc_rows, top_wide)
        picked = jnp.where(lane == rank, doc, picked)
    picked = picked.astype(BF16)
    pairs = clusters // 2
    take_pair = (iota((pairs, clusters), 1) == 2 * iota((pairs, clusters), 0)).astype(BF16)
    doc_ref[...] = jnp.dot(take_pair, picked, preferred_element_type=F32).astype(I32)
    rows = 4 * pairs
    row = iota((rows, clusters), 0)
    spread = (iota((rows, clusters), 1) == 2 * ((row >> 2) ^ flip)).astype(BF16)
    by_row = jnp.dot(spread, picked, preferred_element_type=F32)
    lane_row = iota((rows, 128), 1) == iota((rows, 128), 0) % 4
    doc_of_row = jnp.sum(jnp.where(lane_row, by_row, 0.0), axis=1, keepdims=True).astype(I32)
    pick = (doc_of_row == iota((rows, doc_rows), 1)).astype(BF16)
    copies[2].wait()
    emb = emb_ref[...]
    square = jnp.sum(emb * emb, axis=1, keepdims=True)
    normed = (emb * lax.rsqrt(square + 1e-06)).astype(BF16)
    packed_ref[...] = jnp.dot(pick, normed, preferred_element_type=F32).astype(BF16)


def pack(embeddings, block_ids, counts):
    doc_rows, feature = embeddings.shape
    clusters = block_ids.shape[0]
    return pl.pallas_call(
        pack_kernel,
        out_shape=(
            jax.ShapeDtypeStruct((2 * clusters, feature), BF16),
            jax.ShapeDtypeStruct((clusters // 2, 128), I32),
        ),
        in_specs=[pl.BlockSpec(memory_space=pltpu.HBM)] * 3,
        out_specs=tuple(in_vmem(2)),
        scratch_shapes=[
            pltpu.VMEM(embeddings.shape, F32),
            pltpu.VMEM(block_ids.shape, I32),
            pltpu.VMEM(counts.shape, I32),
            pltpu.SemaphoreType.DMA((3,)),
        ],
        compiler_params=pltpu.CompilerParams(vmem_limit_bytes=24 * MIB),
        name="pack",
    )(embeddings, block_ids, counts)


def label_kernel(ids_hbm, counts_hbm, row_ref, col_ref, ids_ref, counts_ref, sems):
    blocks, block_rows = ids_ref.shape
    chip, core = my_place()
    cluster = 2 * chip_position(chip)
    ids_copy = pltpu.make_async_copy(ids_hbm.at[cluster], ids_ref, sems.at[0])
    counts_copy = pltpu.make_async_copy(counts_hbm, counts_ref, sems.at[1])
    ids_copy.start()
    counts_copy.start()
    group = iota((256, 1), 0)
    of_core = jnp.where(group < 128, core, 1 - core)
    hop = jnp.where(of_core == 0, 4, 1)
    base = owner_chip(group & 63)
    source = jnp.where((group & 64) == 0, base, base ^ hop) * 2 + of_core
    counts_copy.wait()
    counts = counts_ref[...]
    count = jnp.sum(jnp.where(iota(counts.shape, 1) == cluster, counts, 0), axis=1, keepdims=True)
    ids_copy.wait()
    hits = jnp.zeros((256, block_rows), F32)
    for block in range(blocks):
        ids = ids_ref[block : block + 1, :]
        slot_source = jnp.where(block < count, ids >> 8, -1)
        hits = hits + jnp.where(source == slot_source, 1.0, 0.0)
    tally = jnp.sum(hits, axis=1, keepdims=True)
    tally_wide = jnp.broadcast_to(tally, (256, 128)).astype(BF16)
    col_spread = (iota((1024, 256), 0) // 4 == iota((1024, 256), 1)).astype(BF16)
    by_row = jnp.dot(col_spread, tally_wide, preferred_element_type=F32)
    rank = (iota((1024, 128), 0) % 4).astype(F32)
    col = jnp.where(rank >= by_row, 1.0, 0.0)
    col_ref[...] = col
    row_ref[...] = jnp.transpose(col[:512])[:8]


def labels(block_ids, counts):
    return pl.pallas_call(
        label_kernel,
        out_shape=(
            jax.ShapeDtypeStruct((8, 512), F32),
            jax.ShapeDtypeStruct((1024, 128), F32),
        ),
        in_specs=[pl.BlockSpec(memory_space=pltpu.HBM)] * 2,
        out_specs=tuple(in_vmem(2)),
        scratch_shapes=[
            pltpu.VMEM(block_ids.shape[1:], I32),
            pltpu.VMEM(counts.shape, I32),
            pltpu.SemaphoreType.DMA((2,)),
        ],
        compiler_params=pltpu.CompilerParams(vmem_limit_bytes=16 * MIB),
        cost_estimate=pl.CostEstimate(flops=10**9, bytes_accessed=4 * MIB, transcendentals=0),
        name="labels",
    )(block_ids, counts)


def column_best(others, own, other_label, own_label, offset=None):
    scores = lax.dot_general(others, own, (((1,), (1,)), ((), ())), preferred_element_type=F32)
    same = other_label == own_label
    if offset is not None:
        same = same & (iota(scores.shape, 0) + offset != iota(scores.shape, 1))
    return jnp.max(jnp.where(same, scores, -1.0), axis=0, keepdims=True)


def direct_kernel(row_ref, col_ref, direct_ref, direct_other_ref, best_ref):
    own = direct_ref[...]
    label = row_ref[0:1, 0:256]
    best = jnp.maximum(
        column_best(own, own, col_ref[0:256, 0:1], label, 0),
        column_best(direct_other_ref[...], own, col_ref[512:768, 0:1], label),
    )
    best_ref[...] = jnp.broadcast_to(best, best_ref.shape)


def passed_kernel(
    row_ref, col_ref, direct_ref, direct_other_ref, low_ref, high_ref, best_direct_ref, best_ref
):
    passed = jnp.concatenate([low_ref[...], high_ref[...]], axis=0)
    own = jnp.concatenate([direct_ref[...], passed], axis=0)
    best = column_best(passed, own, col_ref[256:512, 0:1], row_ref[0:1, :], 256)
    label = row_ref[0:1, 256:512]
    best_passed = jnp.maximum(
        column_best(direct_ref[...], passed, col_ref[0:256, 0:1], label),
        column_best(direct_other_ref[...], passed, col_ref[512:768, 0:1], label),
    )
    best = jnp.maximum(
        best, jnp.concatenate([best_direct_ref[0:1, :], best_passed], axis=1)
    )
    best_ref[...] = jnp.broadcast_to(best, best_ref.shape)


def final_kernel(
    row_ref, col_ref, direct_ref, low_ref, high_ref, low_other_ref, high_other_ref, best_ref, back_ref
):
    own = jnp.concatenate([direct_ref[...], low_ref[...], high_ref[...]], axis=0)
    others = jnp.concatenate([low_other_ref[...], high_other_ref[...]], axis=0)
    best = column_best(others, own, col_ref[768:1024, 0:1], row_ref[0:1, :])
    best = jnp.maximum(best, best_ref[0:1, :])
    slot, member = iota((128, 512), 0), iota((128, 512), 1)
    spread = jnp.where(member // 4 == slot, jnp.broadcast_to(best, (128, 512)), -1.0)
    for rank in range(4):
        back_ref[:, rank : rank + 1] = jnp.max(
            jnp.where(member % 4 == rank, spread, -1.0), axis=1, keepdims=True
        )


def vmem_call(kernel, shape, name, flops, *operands):
    return pl.pallas_call(
        kernel,
        out_shape=jax.ShapeDtypeStruct(shape, F32),
        in_specs=in_vmem(len(operands)),
        out_specs=in_vmem(1)[0],
        compiler_params=pltpu.CompilerParams(vmem_limit_bytes=16 * MIB),
        cost_estimate=pl.CostEstimate(flops=flops, bytes_accessed=2 * MIB, transcendentals=0),
        name=name,
    )(*operands)


def unpack_kernel(doc_ref, back_ref, out_ref):
    pairs = doc_ref.shape[0]
    doc_rows = out_ref.shape[1]
    doc_lane = iota((pairs, doc_rows), 1)
    top = jnp.full((pairs, doc_rows), -1.0, F32)
    for rank in range(4):
        hit = doc_ref[:, rank : rank + 1] == doc_lane
        top = jnp.maximum(top, jnp.where(hit, back_ref[0:pairs, rank : rank + 1], -1.0))
    out_ref[...] = jnp.max(top, axis=0, keepdims=True)


def chip_routes():
    owners = [owner_chip(position) for position in range(64)]
    direct, passing, back = [], [], []
    low, high = [], []
    for core in range(2):
        near, far = (4, 12) if core == 0 else (1, 3)
        direct.append([chip * 2 + core for chip in owners])
        passing.append([(chip ^ near) * 2 + core for chip in owners])
        back.append(direct[-1] + passing[-1])
        low += [((chip ^ near) * 2 + core, chip * 2 + core) for chip in owners]
        high += [((chip ^ far) * 2 + core, chip * 2 + core) for chip in owners]
    swap = []
    for chip in range(128):
        swap += [(chip * 2, chip * 2 + 1), (chip * 2 + 1, chip * 2)]
    return direct + passing, back, low, high, swap


def body(embeddings, block_ids, block_counts):
    doc_rows, feature = embeddings.shape
    send_groups, back_groups, low_route, high_route, swap = chip_routes()
    embeddings = pltpu.with_memory_space_constraint(embeddings, pltpu.HBM)
    block_ids = pltpu.with_memory_space_constraint(block_ids, pltpu.HBM)
    counts = pltpu.with_memory_space_constraint(block_counts.reshape(1, -1), pltpu.HBM)
    packed, docs = pack(embeddings, block_ids, counts)
    packed = packed.reshape(64, 4, feature)
    direct = lax.all_to_all(
        packed, BOTH, split_axis=0, concat_axis=0, axis_index_groups=send_groups, tiled=True
    )
    direct = lax.optimization_barrier(direct.reshape(256, feature))
    low = lax.ppermute(direct[:128], BOTH, low_route)
    high = lax.ppermute(direct[128:], BOTH, high_route)
    direct_other = lax.ppermute(direct, BOTH, swap)
    row, col = labels(block_ids, counts)
    best = vmem_call(
        direct_kernel, (8, 256), "score_direct", 10**9, row, col, direct, direct_other
    )
    low, high, best = lax.optimization_barrier((low, high, best))
    low_other = lax.ppermute(low, BOTH, swap)
    high_other = lax.ppermute(high, BOTH, swap)
    best = vmem_call(
        passed_kernel, (8, 512), "score_passed", 10**9,
        row, col, direct, direct_other, low, high, best,
    )
    best = vmem_call(
        final_kernel, (128, 4), "score_final", 10**9,
        row, col, direct, low, high, low_other, high_other, best,
    )
    back = lax.all_to_all(
        best, BOTH, split_axis=0, concat_axis=0, axis_index_groups=back_groups, tiled=True
    )
    out = pl.pallas_call(
        unpack_kernel,
        out_shape=jax.ShapeDtypeStruct((1, doc_rows), F32),
        in_specs=in_vmem(2),
        out_specs=in_vmem(1)[0],
        compiler_params=pltpu.CompilerParams(vmem_limit_bytes=4 * MIB),
        name="unpack",
    )(docs, back)
    return out.reshape(doc_rows)


def solution(mesh):
    in_specs = (P(("dp", "pair"), None), P(), P())
    out_specs = P(("dp", "pair"))
    return jax.shard_map(body, mesh=mesh, in_specs=in_specs, out_specs=out_specs, check_vma=False)
```

time: 74.8 us -> 69.9 us (0.934)
  local copies, waits for them, and re-layouts: 3.84 us -> 0.35 us
  starting transfers between devices: 9.49 us -> 7.5 us
    unnamed x10 -> x0, local copies, waits for them, and re-layouts: 3.52 us -> none
    ppermute x3 -> x5, starting transfers between devices: 9.49 us -> 7.5 us  [the longest x1 3.64 us: body(): direct_other = lax.ppermute(direct, BOTH, swap)]
    pallas_call x1, Pallas kernels: 1.73 us -> 2.94 us  [pack(): pl.pallas_call(pack_kernel, out_shape=(jax.ShapeDtypeStruct((2 * clusters...]
    pallas_call x2 -> x4, Pallas kernels: 3.03 us -> 2.57 us  [the longest x3 1.86 us: vmem_call(): pl.pallas_call(kernel, out_shape=jax.ShapeDtypeStruct(shape, F32), in_spe...]
    ppermute x3 -> x5, waiting for transfers between devices: 5.28 us -> 5.11 us  [the longest x1 4.25 us: body(): high = lax.ppermute(direct[128:], BOTH, high_route)]
  transfers between devices with their start and end apart: 3 -> 5, of which waited for: 1 -> 4; matrix products, arithmetic and copies ran while one was open for 0% -> 0% of each run, Pallas kernels for 2% -> 4%
where the time goes in v2:
time: 69.9 us; the launch traced here: 69.6 us
  blocking collectives  49.8 us (71%)
  starting transfers between devices  7.5 us (11%)
  Pallas kernels  6.78 us (10%)
  waiting for transfers between devices  5.11 us (7%)
    all_to_all x1, blocking collectives, body(): lax.all_to_all(packed, BOTH, split_axis=0, concat_axis=0, axis_index_grou...  31.6 us
    all_to_all x1, blocking collectives, body(): lax.all_to_all(best, BOTH, split_axis=0, concat_axis=0, axis_index_groups...  18.2 us
    ppermute x1, waiting for transfers between devices, body(): high = lax.ppermute(direct[128:], BOTH, high_route)  4.25 us
    ppermute x1, starting transfers between devices, body(): direct_other = lax.ppermute(direct, BOTH, swap)  3.64 us
    pallas_call x1, Pallas kernels, pack(): pl.pallas_call(pack_kernel, out_shape=(jax.ShapeDtypeStruct((2 * clusters...  2.94 us
    pallas_call x3, Pallas kernels, vmem_call(): pl.pallas_call(kernel, out_shape=jax.ShapeDtypeStruct(shape, F32), in_spe...  1.86 us
  transfers between devices with their start and end apart: 5, of which 4 were waited for; matrix products, arithmetic and copies ran while one was open for 0% of the time, Pallas kernels for 4%

profile of v2, /device:TPU:1, one launch (start us, length us, event | category | flops | bytes accessed | tf_op | source)
XLA Modules:
  0.0 69.6 jit_solution(12245374743680315622)
XLA Ops:
  0.0 2.9 %pack.1 = (bf16[256,1024]{1,0:T(8,128)(2,1)S(1)}, s32[64,128]{1,0:T(8,128)S(1)}) custom-call(f32[256,1024]{1,0:T(8,128)} %emb_hbm.1, s32[128,2,512]{2,1,0:T(2,128)} %ids_hbm.3, s32[1,128]{1,0:T(1,128)} %bitcast.8), custom_call_target="tpu_custom_call" | custom-call | tf_op jit(solution)/shard_map/pack/pallas_call | solution.py:110
  2.9 0.2 reshape.15
  3.1 31.6 %all_to_all.16 = bf16[64,4,1024]{2,1,0:T(4,128)(2,1)S(1)} all-to-all(bf16[64,4,1024]{2,1,0:T(4,128)(2,1)S(1)} %reshape.15), channel_id=1, replica_groups={{0,4,10,14,16,20,26,30,34,38,40,44,50,54,56,60,64,68,74,78,80,84,90,94,..., dimensions={0} | all-to-all | bytes 1048576 | tf_op jit(solution)/shard_map/all_to_all | solution.py:279
  34.8 0.1 reshape.16.direct_ref
  34.9 3.6 %collective-permute-start.2 = (bf16[256,1024]{1,0:T(8,128)(2,1)S(1)}, bf16[256,1024]{1,0:T(8,128)(2,1)S(1)}, u32[]{:S(2)}, u32[]{:S(2)}) collective-permute-start(bf16[256,1024]{1,0:T(8,128)(2,1)S(1)} %reshape.16.direct_ref), channel_id=1, source_target_pairs={{0,1},{1,0},{2,3},{3,2},{4,5},{5,4},{6,7},{7,6},{8,9},{9,8},{10,11... | collective-permute-start | bytes 1572872 | tf_op jit(solution)/shard_map/ppermute | solution.py:285
  38.6 1.3 %collective-permute-start.1 = (bf16[128,1024]{1,0:T(8,128)(2,1)S(1)}, bf16[128,1024]{1,0:T(8,128)(2,1)S(1)}, u32[]{:S(2)}, u32[]{:S(2)}) collective-permute-start(bf16[128,1024]{1,0:T(8,128)(2,1)S(1)} %get-tuple-element.19), channel_id=1, source_target_pairs={{24,0},{28,4},{18,10},{22,14},{8,16},{12,20},{2,26},{6,30},{58,34}... | collective-permute-start | bytes 786440 | tf_op jit(solution)/shard_map/ppermute | solution.py:284
  39.9 1.3 %collective-permute-start = (bf16[128,1024]{1,0:T(8,128)(2,1)S(1)}, bf16[128,1024]{1,0:T(8,128)(2,1)S(1)}, u32[]{:S(2)}, u32[]{:S(2)}) collective-permute-start(bf16[128,1024]{1,0:T(8,128)(2,1)S(1)} %get-tuple-element.20), channel_id=1, source_target_pairs={{8,0},{12,4},{2,10},{6,14},{24,16},{28,20},{18,26},{22,30},{42,34}... | collective-permute-start | bytes 786440 | tf_op jit(solution)/shard_map/ppermute | solution.py:283
  41.2 1.3 %labels.1 = (f32[8,512]{1,0:T(8,128)S(1)}, f32[1024,128]{1,0:T(8,128)S(1)}) custom-call(s32[128,2,512]{2,1,0:T(2,128)} %ids_hbm.3, s32[1,128]{1,0:T(1,128)} %bitcast.9), custom_call_target="tpu_custom_call" | custom-call | flops 1000000000 | bytes 4194304 | tf_op jit(solution)/shard_map/labels/pallas_call | solution.py:162
  42.4 0.0 collective-permute-done.2.direct_other_ref
  42.5 0.5 score_direct.1.best_direct_ref
  42.9 4.3 %collective-permute-done.1.high_ref = bf16[128,1024]{1,0:T(8,128)(2,1)S(1)} collective-permute-done((bf16[128,1024]{1,0:T(8,128)(2,1)S(1)}, bf16[128,1024]{1,0:T(8,128)(2,1)S(1)}, u32[]{:S(2)}, u32[]{:S(2)}) %collective-permute-start.1) | collective-permute-done | bytes 262176 | tf_op jit(solution)/shard_map/ppermute | solution.py:284
  47.2 0.1 collective-permute-done.low_ref
  47.3 1.3 %collective-permute-start.3 = (bf16[128,1024]{1,0:T(8,128)(2,1)S(1)}, bf16[128,1024]{1,0:T(8,128)(2,1)S(1)}, u32[]{:S(2)}, u32[]{:S(2)}) collective-permute-start(bf16[128,1024]{1,0:T(8,128)(2,1)S(1)} %collective-permute-done.low_ref), channel_id=1, source_target_pairs={{0,1},{1,0},{2,3},{3,2},{4,5},{5,4},{6,7},{7,6},{8,9},{9,8},{10,11... | collective-permute-start | bytes 786440 | tf_op jit(solution)/shard_map/ppermute | solution.py:291
  48.5 0.0 collective-permute-start.4
  48.6 0.8 %score_passed.1.best_ref = f32[8,512]{1,0:T(8,128)S(1)} custom-call(f32[8,512]{1,0:T(8,128)S(1)} %get-tuple-element.13.row_ref, f32[1024,128]{1,0:T(8,128)S(1)} %get-tuple-element.14.col_ref, bf16[256,1024]{1,0:T(8,128)(2,1)S(1)} %reshape.16.direct_ref, bf16[256,1024]{1,0:T(8,128)(2,1)S(1)} %collective-permute-done.2.direct_other_ref, ...), custom_call_target="tpu_custom_call" | custom-call | flops 1000000000 | bytes 2097152 | tf_op jit(solution)/shard_map/score_passed/pallas_call | solution.py:232
  49.3 0.4 collective-permute-done.3.low_other_ref
  49.7 0.4 collective-permute-done.4.high_other_ref
  50.1 0.6 score_final.1
  50.7 18.2 %all_to_all.17 = f32[128,1,4]{2,1,0:T(1,128)S(1)} all-to-all(f32[128,1,4]{2,1,0:T(1,128)S(1)} %bitcast.7), channel_id=1, replica_groups={{0,4,10,14,16,20,26,30,34,38,40,44,50,54,56,60,64,68,74,78,80,84,90,94,..., dimensions={0} | all-to-all | bytes 4096 | tf_op jit(solution)/shard_map/all_to_all | solution.py:301
  68.9 0.7 %unpack.1 = f32[1,256]{1,0:T(1,128)} custom-call(s32[64,128]{1,0:T(8,128)S(1)} %get-tuple-element.12.doc_ref, f32[128,4]{1,0:T(8,128)S(1)} %bitcast.6), custom_call_target="tpu_custom_call" | custom-call | tf_op jit(solution)/shard_map/unpack/pallas_call | solution.py:304
  (1 shorter events, 0.0 us)
Async XLA Ops:
  34.9 7.6 %collective-permute-start.2 = (bf16[256,1024]{1,0:T(8,128)(2,1)S(1)}, bf16[256,1024]{1,0:T(8,128)(2,1)S(1)}, u32[]{:S(2)}, u32[]{:S(2)}) collective-permute-start(bf16[256,1024]{1,0:T(8,128)(2,1)S(1)} %reshape.16.direct_ref), channel_id=1, source_target_pairs={{0,1},{1,0},{2,3},{3,2},{4,5},{5,4},{6,7},{7,6},{8,9},{9,8},{10,11... | collective-permute-start | bytes 1572872 | tf_op jit(solution)/shard_map/ppermute | solution.py:285
  38.6 8.6 %collective-permute-start.1 = (bf16[128,1024]{1,0:T(8,128)(2,1)S(1)}, bf16[128,1024]{1,0:T(8,128)(2,1)S(1)}, u32[]{:S(2)}, u32[]{:S(2)}) collective-permute-start(bf16[128,1024]{1,0:T(8,128)(2,1)S(1)} %get-tuple-element.19), channel_id=1, source_target_pairs={{24,0},{28,4},{18,10},{22,14},{8,16},{12,20},{2,26},{6,30},{58,34}... | collective-permute-start | bytes 786440 | tf_op jit(solution)/shard_map/ppermute | solution.py:284
  39.9 7.4 %collective-permute-start = (bf16[128,1024]{1,0:T(8,128)(2,1)S(1)}, bf16[128,1024]{1,0:T(8,128)(2,1)S(1)}, u32[]{:S(2)}, u32[]{:S(2)}) collective-permute-start(bf16[128,1024]{1,0:T(8,128)(2,1)S(1)} %get-tuple-element.20), channel_id=1, source_target_pairs={{8,0},{12,4},{2,10},{6,14},{24,16},{28,20},{18,26},{22,30},{42,34}... | collective-permute-start | bytes 786440 | tf_op jit(solution)/shard_map/ppermute | solution.py:283
  47.3 2.4 %collective-permute-start.3 = (bf16[128,1024]{1,0:T(8,128)(2,1)S(1)}, bf16[128,1024]{1,0:T(8,128)(2,1)S(1)}, u32[]{:S(2)}, u32[]{:S(2)}) collective-permute-start(bf16[128,1024]{1,0:T(8,128)(2,1)S(1)} %collective-permute-done.low_ref), channel_id=1, source_target_pairs={{0,1},{1,0},{2,3},{3,2},{4,5},{5,4},{6,7},{7,6},{8,9},{9,8},{10,11... | collective-permute-start | bytes 786440 | tf_op jit(solution)/shard_map/ppermute | solution.py:291
  48.5 1.5 %collective-permute-start.4 = (bf16[128,1024]{1,0:T(8,128)(2,1)S(1)}, bf16[128,1024]{1,0:T(8,128)(2,1)S(1)}, u32[]{:S(2)}, u32[]{:S(2)}) collective-permute-start(bf16[128,1024]{1,0:T(8,128)(2,1)S(1)} %collective-permute-done.1.high_ref), channel_id=1, source_target_pairs={{0,1},{1,0},{2,3},{3,2},{4,5},{5,4},{6,7},{7,6},{8,9},{9,8},{10,11... | collective-permute-start | bytes 786440 | tf_op jit(solution)/shard_map/ppermute | solution.py:292

commit v3 on v2

--- a/solution.py
+++ b/solution.py
@@ -12,6 +12,7 @@
 I32 = jnp.int32
 MIB = 1024 * 1024
 BOTH = ("dp", "pair")
+LOW = 24
 
 
 def iota(shape, dim):
@@ -36,6 +37,20 @@
 
 def owner_chip(position):
     return 2 * position + (((position >> 3) + (position >> 1)) & 1)
+
+
+def merge_twos(a, b):
+    low, high = jnp.minimum(a[0], b[0]), jnp.maximum(a[1], b[1])
+    return [
+        jnp.maximum(a[0], b[0]), jnp.maximum(low, high), jnp.minimum(low, high), jnp.minimum(a[1], b[1])
+    ]
+
+
+def top_four(a, b):
+    c = [jnp.maximum(x, y) for x, y in zip(a, b[::-1])]
+    e, f = jnp.maximum(c[0], c[2]), jnp.maximum(c[1], c[3])
+    g, h = jnp.minimum(c[0], c[2]), jnp.minimum(c[1], c[3])
+    return [jnp.maximum(e, f), jnp.minimum(e, f), jnp.maximum(g, h), jnp.minimum(g, h)]
 
 
 def pack_kernel(
@@ -49,16 +64,15 @@
     for copy in copies:
         copy.start()
     doc_rows = emb_ref.shape[0]
-    clusters, blocks, block_rows = ids_ref.shape
+    clusters = ids_ref.shape[0] // 8
     doc_total = doc_rows * 2 * clusters
     chip, core = my_place()
     first = (chip * 2 + core) * doc_rows
-    turned = (chip_parity(chip) == 1) & (chip >= clusters // 2)
+    turned = (chip_parity(chip) == 1) & (chip_position(chip) >= LOW)
     flip = jnp.where(turned, jnp.where(core == 0, 4, 1), 0)
     diagonal = iota((clusters, clusters), 0) == iota((clusters, clusters), 1)
     even = iota((clusters, 1), 0) % 2 == 0
     lift = jnp.where(even, doc_rows, 0)
-    lane = iota((clusters, 128), 1)
     even_wide = iota((clusters, 128), 0) % 2 == 0
     copies[0].wait()
     counts = jnp.sum(
@@ -67,50 +81,66 @@
         keepdims=True,
     )
     copies[1].wait()
-    keys = []
-    for block in range(blocks):
-        ids = ids_ref[:, block, :]
+    tiles = []
+    for tile in range(8):
+        ids = ids_ref[pl.ds(tile, clusters, stride=8), :]
         local = ids - first
-        mine = (local >= 0) & (local < doc_rows) & (block < counts) & (ids < doc_total)
-        keys.append(jnp.where(mine, local + lift, -1).astype(F32))
-    picked = jnp.zeros((clusters, 128), F32)
+        mine = (local >= 0) & (local < doc_rows) & (tile % 2 < counts) & (ids < doc_total)
+        tiles.append(jnp.where(mine, local + lift, -1).astype(F32))
+    twos = [(jnp.maximum(a, b), jnp.minimum(a, b)) for a, b in zip(tiles[::2], tiles[1::2])]
+    fours = [merge_twos(a, b) for a, b in zip(twos[::2], twos[1::2])]
+    mine_top = top_four(*fours)
+    partner_top = [
+        jnp.where(even_wide, pltpu.roll(a, clusters - 1, 0), pltpu.roll(a, 1, 0)) for a in mine_top
+    ]
+    ranked = top_four(mine_top, partner_top)
+    ranked = [jnp.transpose(a) for a in ranked]
+    doc_column = iota((doc_rows, clusters), 0).astype(F32)
+    which = iota((clusters, clusters), 0)
+    picked = jnp.zeros((clusters, clusters), F32)
+    hits = []
     for rank in range(4):
-        best = jnp.max(jnp.maximum(keys[0], keys[1]), axis=1, keepdims=True)
-        wide = jnp.broadcast_to(best, (clusters, 128))
-        other = jnp.where(
-            even_wide, pltpu.roll(wide, clusters - 1, 0), pltpu.roll(wide, 1, 0)
-        )
-        top_wide = jnp.maximum(wide, other)
-        top = top_wide[:, :1]
-        if rank < 3:
-            keys = [jnp.where(key == top, -1.0, key) for key in keys]
-        doc = jnp.where(top_wide >= doc_rows, top_wide - doc_rows, top_wide)
-        picked = jnp.where(lane == rank, doc, picked)
-    picked = picked.astype(BF16)
+        top = jnp.max(ranked[0], axis=0, keepdims=True)
+        hit = ranked[0] == top
+        ranked = [jnp.where(hit, b, a) for a, b in zip(ranked, ranked[1:])]
+        doc = jnp.where(top >= doc_rows, top - doc_rows, top)
+        picked = jnp.where(which == rank, doc, picked)
+        hits.append((doc == doc_column).astype(BF16))
     pairs = clusters // 2
+    rows = 4 * pairs
+    row, spot = iota((rows, 4 * clusters), 0), iota((rows, 4 * clusters), 1)
+    spread = (spot == (row & 3) * clusters + 2 * ((row >> 2) ^ flip)).astype(BF16)
+    last = (((1,), (1,)), ((), ()))
+    pick = lax.dot_general(
+        spread, jnp.concatenate(hits, axis=1), last, preferred_element_type=F32
+    ).astype(BF16)
     take_pair = (iota((pairs, clusters), 1) == 2 * iota((pairs, clusters), 0)).astype(BF16)
-    doc_ref[...] = jnp.dot(take_pair, picked, preferred_element_type=F32).astype(I32)
-    rows = 4 * pairs
-    row = iota((rows, clusters), 0)
-    spread = (iota((rows, clusters), 1) == 2 * ((row >> 2) ^ flip)).astype(BF16)
-    by_row = jnp.dot(spread, picked, preferred_element_type=F32)
-    lane_row = iota((rows, 128), 1) == iota((rows, 128), 0) % 4
-    doc_of_row = jnp.sum(jnp.where(lane_row, by_row, 0.0), axis=1, keepdims=True).astype(I32)
-    pick = (doc_of_row == iota((rows, doc_rows), 1)).astype(BF16)
+    doc_ref[...] = lax.dot_general(
+        take_pair, picked.astype(BF16), last, preferred_element_type=F32
+    ).astype(I32)
     copies[2].wait()
     emb = emb_ref[...]
     square = jnp.sum(emb * emb, axis=1, keepdims=True)
     normed = (emb * lax.rsqrt(square + 1e-06)).astype(BF16)
-    packed_ref[...] = jnp.dot(pick, normed, preferred_element_type=F32).astype(BF16)
+    packed = jnp.dot(pick, normed, preferred_element_type=F32).astype(BF16)
+    packed_ref[...] = packed.reshape(packed_ref.shape)
+
+
+def in_hbm(array):
+    return pltpu.with_memory_space_constraint(array, pltpu.HBM)
 
 
 def pack(embeddings, block_ids, counts):
+    clusters, blocks, block_rows = block_ids.shape
+    tiles = block_rows // 128
+    block_ids = block_ids.reshape(clusters, blocks, tiles, 128).transpose(0, 2, 1, 3)
+    block_ids = block_ids.reshape(clusters * tiles * blocks, 128)
+    embeddings, block_ids, counts = in_hbm(embeddings), in_hbm(block_ids), in_hbm(counts)
     doc_rows, feature = embeddings.shape
-    clusters = block_ids.shape[0]
     return pl.pallas_call(
         pack_kernel,
         out_shape=(
-            jax.ShapeDtypeStruct((2 * clusters, feature), BF16),
+            jax.ShapeDtypeStruct((clusters // 2, 4, feature), BF16),
             jax.ShapeDtypeStruct((clusters // 2, 128), I32),
         ),
         in_specs=[pl.BlockSpec(memory_space=pltpu.HBM)] * 3,
@@ -159,6 +189,7 @@
 
 
 def labels(block_ids, counts):
+    block_ids, counts = in_hbm(block_ids), in_hbm(counts)
     return pl.pallas_call(
         label_kernel,
         out_shape=(
@@ -186,27 +217,27 @@
     return jnp.max(jnp.where(same, scores, -1.0), axis=0, keepdims=True)
 
 
-def direct_kernel(row_ref, col_ref, direct_ref, direct_other_ref, best_ref):
-    own = direct_ref[...]
-    label = row_ref[0:1, 0:256]
-    best = jnp.maximum(
-        column_best(own, own, col_ref[0:256, 0:1], label, 0),
-        column_best(direct_other_ref[...], own, col_ref[512:768, 0:1], label),
-    )
+def rows_of(*refs):
+    rows = [ref[...].reshape(4 * ref.shape[0], ref.shape[2]) for ref in refs]
+    return rows[0] if len(rows) == 1 else jnp.concatenate(rows, axis=0)
+
+
+def direct_kernel(row_ref, col_ref, direct_ref, best_ref):
+    own = rows_of(direct_ref)
+    best = column_best(own, own, col_ref[0:256, 0:1], row_ref[0:1, 0:256], 0)
     best_ref[...] = jnp.broadcast_to(best, best_ref.shape)
 
 
 def passed_kernel(
     row_ref, col_ref, direct_ref, direct_other_ref, low_ref, high_ref, best_direct_ref, best_ref
 ):
-    passed = jnp.concatenate([low_ref[...], high_ref[...]], axis=0)
-    own = jnp.concatenate([direct_ref[...], passed], axis=0)
-    best = column_best(passed, own, col_ref[256:512, 0:1], row_ref[0:1, :], 256)
-    label = row_ref[0:1, 256:512]
-    best_passed = jnp.maximum(
-        column_best(direct_ref[...], passed, col_ref[0:256, 0:1], label),
-        column_best(direct_other_ref[...], passed, col_ref[512:768, 0:1], label),
-    )
+    direct, passed = rows_of(direct_ref), rows_of(low_ref, high_ref)
+    own = jnp.concatenate([direct, passed], axis=0)
+    best = jnp.maximum(
+        column_best(passed, own, col_ref[256:512, 0:1], row_ref[0:1, :], 256),
+        column_best(rows_of(direct_other_ref), own, col_ref[512:768, 0:1], row_ref[0:1, :]),
+    )
+    best_passed = column_best(direct, passed, col_ref[0:256, 0:1], row_ref[0:1, 256:512])
     best = jnp.maximum(
         best, jnp.concatenate([best_direct_ref[0:1, :], best_passed], axis=1)
     )
@@ -216,8 +247,8 @@
 def final_kernel(
     row_ref, col_ref, direct_ref, low_ref, high_ref, low_other_ref, high_other_ref, best_ref, back_ref
 ):
-    own = jnp.concatenate([direct_ref[...], low_ref[...], high_ref[...]], axis=0)
-    others = jnp.concatenate([low_other_ref[...], high_other_ref[...]], axis=0)
+    own = rows_of(direct_ref, low_ref, high_ref)
+    others = rows_of(low_other_ref, high_other_ref)
     best = column_best(others, own, col_ref[768:1024, 0:1], row_ref[0:1, :])
     best = jnp.maximum(best, best_ref[0:1, :])
     slot, member = iota((128, 512), 0), iota((128, 512), 1)
@@ -262,34 +293,29 @@
         back.append(direct[-1] + passing[-1])
         low += [((chip ^ near) * 2 + core, chip * 2 + core) for chip in owners]
         high += [((chip ^ far) * 2 + core, chip * 2 + core) for chip in owners]
-    swap = []
-    for chip in range(128):
-        swap += [(chip * 2, chip * 2 + 1), (chip * 2 + 1, chip * 2)]
-    return direct + passing, back, low, high, swap
+    swap = [(device, device ^ 1) for device in range(256)]
+    owner_swap = [(device, device ^ 1) for device in range(256) if chip_parity(device // 2) == 0]
+    return direct + passing, back, low, high, swap, owner_swap
 
 
 def body(embeddings, block_ids, block_counts):
-    doc_rows, feature = embeddings.shape
-    send_groups, back_groups, low_route, high_route, swap = chip_routes()
-    embeddings = pltpu.with_memory_space_constraint(embeddings, pltpu.HBM)
-    block_ids = pltpu.with_memory_space_constraint(block_ids, pltpu.HBM)
-    counts = pltpu.with_memory_space_constraint(block_counts.reshape(1, -1), pltpu.HBM)
+    doc_rows = embeddings.shape[0]
+    send_groups, back_groups, low_route, high_route, swap, owner_swap = chip_routes()
+    counts = block_counts.reshape(1, -1)
     packed, docs = pack(embeddings, block_ids, counts)
-    packed = packed.reshape(64, 4, feature)
     direct = lax.all_to_all(
         packed, BOTH, split_axis=0, concat_axis=0, axis_index_groups=send_groups, tiled=True
     )
-    direct = lax.optimization_barrier(direct.reshape(256, feature))
-    low = lax.ppermute(direct[:128], BOTH, low_route)
-    high = lax.ppermute(direct[128:], BOTH, high_route)
+    high = lax.ppermute(direct[LOW:], BOTH, high_route)
+    low = lax.ppermute(direct[:LOW], BOTH, low_route)
+    late_ids, late_counts, direct = lax.optimization_barrier((block_ids, counts, direct))
+    row, col = labels(late_ids, late_counts)
     direct_other = lax.ppermute(direct, BOTH, swap)
-    row, col = labels(block_ids, counts)
-    best = vmem_call(
-        direct_kernel, (8, 256), "score_direct", 10**9, row, col, direct, direct_other
-    )
-    low, high, best = lax.optimization_barrier((low, high, best))
-    low_other = lax.ppermute(low, BOTH, swap)
-    high_other = lax.ppermute(high, BOTH, swap)
+    best = vmem_call(direct_kernel, (8, 256), "score_direct", 10**9, row, col, direct)
+    high, best = lax.optimization_barrier((high, best))
+    high_other = lax.ppermute(high, BOTH, owner_swap)
+    low, best = lax.optimization_barrier((low, best))
+    low_other = lax.ppermute(low, BOTH, owner_swap)
     best = vmem_call(
         passed_kernel, (8, 512), "score_passed", 10**9,
         row, col, direct, direct_other, low, high, best,

time: 69.9 us -> 72.1 us (1.031)
  starting transfers between devices: 7.5 us -> 14.7 us
  waiting for transfers between devices: 5.11 us -> 1.58 us
  blocking collectives: 49.8 us -> 49 us
    ppermute x4, starting transfers between devices: 3.86 us -> 11.1 us  [the longest x1 6.6 us: body(): high_other = lax.ppermute(high, BOTH, owner_swap)]
    ppermute x4, waiting for transfers between devices: 5.1 us -> 1.58 us  [the longest x1 1.09 us: body(): high = lax.ppermute(direct[LOW:], BOTH, high_route)]
    all_to_all x1, blocking collectives: 18.2 us -> 17.4 us  [body(): lax.all_to_all(best, BOTH, split_axis=0, concat_axis=0, axis_index_groups...]
  transfers between devices with their start and end apart: 5 -> 5, of which waited for: 4 -> 2; matrix products, arithmetic and copies ran while one was open for 0% -> 0% of each run, Pallas kernels for 4% -> 4%
where the time goes in v3:
time: 72.1 us; the launch traced here: 71.8 us
  blocking collectives  49 us (68%)
  starting transfers between devices  14.7 us (20%)
  Pallas kernels  6.23 us (9%)
  waiting for transfers between devices  1.58 us (2%)
    all_to_all x1, blocking collectives, body(): lax.all_to_all(packed, BOTH, split_axis=0, concat_axis=0, axis_index_grou...  31.6 us
    all_to_all x1, blocking collectives, body(): lax.all_to_all(best, BOTH, split_axis=0, concat_axis=0, axis_index_groups...  17.4 us
    ppermute x1, starting transfers between devices, body(): high_other = lax.ppermute(high, BOTH, owner_swap)  6.6 us
    ppermute x1, starting transfers between devices, body(): direct_other = lax.ppermute(direct, BOTH, swap)  3.64 us
    pallas_call x1, Pallas kernels, pack(): pl.pallas_call(pack_kernel, out_shape=(jax.ShapeDtypeStruct((clusters //...  2.36 us
    ppermute x1, starting transfers between devices, body(): low_other = lax.ppermute(low, BOTH, owner_swap)  1.92 us
    pallas_call x3, Pallas kernels, vmem_call(): pl.pallas_call(kernel, out_shape=jax.ShapeDtypeStruct(shape, F32), in_spe...  1.9 us
  transfers between devices with their start and end apart: 5, of which 2 were waited for; matrix products, arithmetic and copies ran while one was open for 0% of the time, Pallas kernels for 4%

profile of v3, /device:TPU:1, one launch (start us, length us, event | category | flops | bytes accessed | tf_op | source)
XLA Modules:
  0.0 71.8 jit_solution(9189593387255696248)
XLA Ops:
  0.0 2.4 %pack.1 = (bf16[64,4,1024]{2,1,0:T(4,128)(2,1)S(1)}, s32[64,128]{1,0:T(8,128)S(1)}) custom-call(f32[256,1024]{1,0:T(8,128)} %emb_hbm.1, s32[1024,128]{1,0:T(8,128)} %bitcast.13, s32[1,128]{1,0:T(1,128)} %bitcast.14), custom_call_target="tpu_custom_call" | custom-call | tf_op jit(solution)/shard_map/pack/pallas_call | solution.py:140
  2.4 31.6 %all_to_all.16.direct_ref = bf16[64,4,1024]{2,1,0:T(4,128)(2,1)S(1)} all-to-all(bf16[64,4,1024]{2,1,0:T(4,128)(2,1)S(1)} %get-tuple-element.17), channel_id=1, replica_groups={{0,4,10,14,16,20,26,30,34,38,40,44,50,54,56,60,64,68,74,78,80,84,90,94,..., dimensions={0} | all-to-all | bytes 1048576 | tf_op jit(solution)/shard_map/all_to_all | solution.py:306
  34.0 0.1 slice.9
  34.1 1.3 %collective-permute-start.1 = (bf16[40,4,1024]{2,1,0:T(4,128)(2,1)S(1)}, bf16[40,4,1024]{2,1,0:T(4,128)(2,1)S(1)}, u32[]{:S(2)}, u32[]{:S(2)}) collective-permute-start(bf16[40,4,1024]{2,1,0:T(4,128)(2,1)S(1)} %slice.9), channel_id=1, source_target_pairs={{24,0},{28,4},{18,10},{22,14},{8,16},{12,20},{2,26},{6,30},{58,34}... | collective-permute-start | bytes 983048 | tf_op jit(solution)/shard_map/ppermute | solution.py:309
  35.4 3.6 %collective-permute-start.4 = (bf16[64,4,1024]{2,1,0:T(4,128)(2,1)S(1)}, bf16[64,4,1024]{2,1,0:T(4,128)(2,1)S(1)}, u32[]{:S(2)}, u32[]{:S(2)}) collective-permute-start(bf16[64,4,1024]{2,1,0:T(4,128)(2,1)S(1)} %all_to_all.16.direct_ref), channel_id=1, source_target_pairs={{0,1},{1,0},{2,3},{3,2},{4,5},{5,4},{6,7},{7,6},{8,9},{9,8},{10,11... | collective-permute-start | bytes 1572872 | tf_op jit(solution)/shard_map/ppermute | solution.py:313
  39.0 0.1 slice.8
  39.1 1.3 %collective-permute-start = (bf16[24,4,1024]{2,1,0:T(4,128)(2,1)S(1)}, bf16[24,4,1024]{2,1,0:T(4,128)(2,1)S(1)}, u32[]{:S(2)}, u32[]{:S(2)}) collective-permute-start(bf16[24,4,1024]{2,1,0:T(4,128)(2,1)S(1)} %slice.8), channel_id=1, source_target_pairs={{8,0},{12,4},{2,10},{6,14},{24,16},{28,20},{18,26},{22,30},{42,34}... | collective-permute-start | bytes 589832 | tf_op jit(solution)/shard_map/ppermute | solution.py:310
  40.4 1.3 %labels.1 = (f32[8,512]{1,0:T(8,128)S(1)}, f32[1024,128]{1,0:T(8,128)S(1)}) custom-call(s32[128,2,512]{2,1,0:T(2,128)} %ids_hbm, s32[1,128]{1,0:T(1,128)} %bitcast.15), custom_call_target="tpu_custom_call" | custom-call | flops 1000000000 | bytes 4194304 | tf_op jit(solution)/shard_map/labels/pallas_call | solution.py:193
  41.7 0.3 score_direct.1.best_direct_ref
  42.0 1.1 %collective-permute-done.1.high_ref = bf16[40,4,1024]{2,1,0:T(4,128)(2,1)S(1)} collective-permute-done((bf16[40,4,1024]{2,1,0:T(4,128)(2,1)S(1)}, bf16[40,4,1024]{2,1,0:T(4,128)(2,1)S(1)}, u32[]{:S(2)}, u32[]{:S(2)}) %collective-permute-start.1) | collective-permute-done | bytes 327712 | tf_op jit(solution)/shard_map/ppermute | solution.py:309
  43.1 6.6 %collective-permute-start.3 = (bf16[40,4,1024]{2,1,0:T(4,128)(2,1)S(1)}, bf16[40,4,1024]{2,1,0:T(4,128)(2,1)S(1)}, u32[]{:S(2)}, u32[]{:S(2)}) collective-permute-start(bf16[40,4,1024]{2,1,0:T(4,128)(2,1)S(1)} %collective-permute-done.1.high_ref), channel_id=1, source_target_pairs={{0,1},{1,0},{4,5},{5,4},{10,11},{11,10},{14,15},{15,14},{16,17},{1... | collective-permute-start | bytes 983048 | tf_op jit(solution)/shard_map/ppermute | solution.py:316
  49.7 0.0 collective-permute-done.low_ref
  49.7 1.9 %collective-permute-start.2 = (bf16[24,4,1024]{2,1,0:T(4,128)(2,1)S(1)}, bf16[24,4,1024]{2,1,0:T(4,128)(2,1)S(1)}, u32[]{:S(2)}, u32[]{:S(2)}) collective-permute-start(bf16[24,4,1024]{2,1,0:T(4,128)(2,1)S(1)} %collective-permute-done.low_ref), channel_id=1, source_target_pairs={{0,1},{1,0},{4,5},{5,4},{10,11},{11,10},{14,15},{15,14},{16,17},{1... | collective-permute-start | bytes 589832 | tf_op jit(solution)/shard_map/ppermute | solution.py:318
  51.7 0.0 collective-permute-done.4.direct_other_ref
  51.7 0.9 %score_passed.1.best_ref = f32[8,512]{1,0:T(8,128)S(1)} custom-call(f32[8,512]{1,0:T(8,128)S(1)} %get-tuple-element.20.row_ref, f32[1024,128]{1,0:T(8,128)S(1)} %get-tuple-element.21.col_ref, bf16[64,4,1024]{2,1,0:T(4,128)(2,1)S(1)} %all_to_all.16.direct_ref, bf16[64,4,1024]{2,1,0:T(4,128)(2,1)S(1)} %collective-permute-done.4.direct_other_ref, ...), custom_call_target="tpu_custom_call" | custom-call | flops 1000000000 | bytes 2097152 | tf_op jit(solution)/shard_map/score_passed/pallas_call | solution.py:263
  52.6 0.5 collective-permute-done.2.low_other_ref
  53.1 0.0 collective-permute-done.3.high_other_ref
  53.1 0.6 score_final.1
  53.7 17.4 %all_to_all.17 = f32[128,1,4]{2,1,0:T(1,128)S(1)} all-to-all(f32[128,1,4]{2,1,0:T(1,128)S(1)} %bitcast.12), channel_id=1, replica_groups={{0,4,10,14,16,20,26,30,34,38,40,44,50,54,56,60,64,68,74,78,80,84,90,94,..., dimensions={0} | all-to-all | bytes 4096 | tf_op jit(solution)/shard_map/all_to_all | solution.py:327
  71.1 0.7 unpack.1
Async XLA Ops:
  34.1 9.0 %collective-permute-start.1 = (bf16[40,4,1024]{2,1,0:T(4,128)(2,1)S(1)}, bf16[40,4,1024]{2,1,0:T(4,128)(2,1)S(1)}, u32[]{:S(2)}, u32[]{:S(2)}) collective-permute-start(bf16[40,4,1024]{2,1,0:T(4,128)(2,1)S(1)} %slice.9), channel_id=1, source_target_pairs={{24,0},{28,4},{18,10},{22,14},{8,16},{12,20},{2,26},{6,30},{58,34}... | collective-permute-start | bytes 983048 | tf_op jit(solution)/shard_map/ppermute | solution.py:309
  35.4 16.3 %collective-permute-start.4 = (bf16[64,4,1024]{2,1,0:T(4,128)(2,1)S(1)}, bf16[64,4,1024]{2,1,0:T(4,128)(2,1)S(1)}, u32[]{:S(2)}, u32[]{:S(2)}) collective-permute-start(bf16[64,4,1024]{2,1,0:T(4,128)(2,1)S(1)} %all_to_all.16.direct_ref), channel_id=1, source_target_pairs={{0,1},{1,0},{2,3},{3,2},{4,5},{5,4},{6,7},{7,6},{8,9},{9,8},{10,11... | collective-permute-start | bytes 1572872 | tf_op jit(solution)/shard_map/ppermute | solution.py:313
  39.1 10.6 %collective-permute-start = (bf16[24,4,1024]{2,1,0:T(4,128)(2,1)S(1)}, bf16[24,4,1024]{2,1,0:T(4,128)(2,1)S(1)}, u32[]{:S(2)}, u32[]{:S(2)}) collective-permute-start(bf16[24,4,1024]{2,1,0:T(4,128)(2,1)S(1)} %slice.8), channel_id=1, source_target_pairs={{8,0},{12,4},{2,10},{6,14},{24,16},{28,20},{18,26},{22,30},{42,34}... | collective-permute-start | bytes 589832 | tf_op jit(solution)/shard_map/ppermute | solution.py:310
  43.1 10.0 %collective-permute-start.3 = (bf16[40,4,1024]{2,1,0:T(4,128)(2,1)S(1)}, bf16[40,4,1024]{2,1,0:T(4,128)(2,1)S(1)}, u32[]{:S(2)}, u32[]{:S(2)}) collective-permute-start(bf16[40,4,1024]{2,1,0:T(4,128)(2,1)S(1)} %collective-permute-done.1.high_ref), channel_id=1, source_target_pairs={{0,1},{1,0},{4,5},{5,4},{10,11},{11,10},{14,15},{15,14},{16,17},{1... | collective-permute-start | bytes 983048 | tf_op jit(solution)/shard_map/ppermute | solution.py:316
  49.7 3.3 %collective-permute-start.2 = (bf16[24,4,1024]{2,1,0:T(4,128)(2,1)S(1)}, bf16[24,4,1024]{2,1,0:T(4,128)(2,1)S(1)}, u32[]{:S(2)}, u32[]{:S(2)}) collective-permute-start(bf16[24,4,1024]{2,1,0:T(4,128)(2,1)S(1)} %collective-permute-done.low_ref), channel_id=1, source_target_pairs={{0,1},{1,0},{4,5},{5,4},{10,11},{11,10},{14,15},{15,14},{16,17},{1... | collective-permute-start | bytes 589832 | tf_op jit(solution)/shard_map/ppermute | solution.py:318

commit v4 on v3

--- a/solution.py
+++ b/solution.py
@@ -222,9 +222,13 @@
     return rows[0] if len(rows) == 1 else jnp.concatenate(rows, axis=0)
 
 
-def direct_kernel(row_ref, col_ref, direct_ref, best_ref):
+def direct_kernel(row_ref, col_ref, direct_ref, direct_other_ref, best_ref):
     own = rows_of(direct_ref)
-    best = column_best(own, own, col_ref[0:256, 0:1], row_ref[0:1, 0:256], 0)
+    label = row_ref[0:1, 0:256]
+    best = jnp.maximum(
+        column_best(own, own, col_ref[0:256, 0:1], label, 0),
+        column_best(rows_of(direct_other_ref), own, col_ref[512:768, 0:1], label),
+    )
     best_ref[...] = jnp.broadcast_to(best, best_ref.shape)
 
 
@@ -233,11 +237,12 @@
 ):
     direct, passed = rows_of(direct_ref), rows_of(low_ref, high_ref)
     own = jnp.concatenate([direct, passed], axis=0)
-    best = jnp.maximum(
-        column_best(passed, own, col_ref[256:512, 0:1], row_ref[0:1, :], 256),
-        column_best(rows_of(direct_other_ref), own, col_ref[512:768, 0:1], row_ref[0:1, :]),
-    )
-    best_passed = column_best(direct, passed, col_ref[0:256, 0:1], row_ref[0:1, 256:512])
+    best = column_best(passed, own, col_ref[256:512, 0:1], row_ref[0:1, :], 256)
+    label = row_ref[0:1, 256:512]
+    best_passed = jnp.maximum(
+        column_best(direct, passed, col_ref[0:256, 0:1], label),
+        column_best(rows_of(direct_other_ref), passed, col_ref[512:768, 0:1], label),
+    )
     best = jnp.maximum(
         best, jnp.concatenate([best_direct_ref[0:1, :], best_passed], axis=1)
     )
@@ -311,11 +316,12 @@
     late_ids, late_counts, direct = lax.optimization_barrier((block_ids, counts, direct))
     row, col = labels(late_ids, late_counts)
     direct_other = lax.ppermute(direct, BOTH, swap)
-    best = vmem_call(direct_kernel, (8, 256), "score_direct", 10**9, row, col, direct)
-    high, best = lax.optimization_barrier((high, best))
+    best = vmem_call(
+        direct_kernel, (8, 256), "score_direct", 10**9, row, col, direct, direct_other
+    )
+    low, high, best = lax.optimization_barrier((low, high, best))
+    low_other = lax.ppermute(low, BOTH, owner_swap)
     high_other = lax.ppermute(high, BOTH, owner_swap)
-    low, best = lax.optimization_barrier((low, best))
-    low_other = lax.ppermute(low, BOTH, owner_swap)
     best = vmem_call(
         passed_kernel, (8, 512), "score_passed", 10**9,
         row, col, direct, direct_other, low, high, best,

time: 72.1 us -> 72.1 us (level)
  waiting for transfers between devices: 1.58 us -> 5.51 us
  starting transfers between devices: 14.7 us -> 10.8 us
    ppermute x1, starting transfers between devices: 6.6 us -> 2.76 us  [body(): high_other = lax.ppermute(high, BOTH, owner_swap)]
    ppermute x1, waiting for transfers between devices: 0.01 us -> 3.64 us  [body(): low = lax.ppermute(direct[:LOW], BOTH, low_route)]
  transfers between devices with their start and end apart: 5 -> 5, of which waited for: 2 -> 3; matrix products, arithmetic and copies ran while one was open for 0% -> 0% of each run, Pallas kernels for 4% -> 4%
where the time goes in v4:
time: 72.1 us; the launch traced here: 71.8 us
  blocking collectives  49 us (68%)
  starting transfers between devices  10.8 us (15%)
  Pallas kernels  6.22 us (9%)
  waiting for transfers between devices  5.51 us (8%)
    all_to_all x1, blocking collectives, body(): lax.all_to_all(packed, BOTH, split_axis=0, concat_axis=0, axis_index_grou...  31.6 us
    all_to_all x1, blocking collectives, body(): lax.all_to_all(best, BOTH, split_axis=0, concat_axis=0, axis_index_groups...  17.4 us
    ppermute x1, waiting for transfers between devices, body(): low = lax.ppermute(direct[:LOW], BOTH, low_route)  3.64 us
    ppermute x1, starting transfers between devices, body(): direct_other = lax.ppermute(direct, BOTH, swap)  3.55 us
    ppermute x1, starting transfers between devices, body(): high_other = lax.ppermute(high, BOTH, owner_swap)  2.76 us
    pallas_call x1, Pallas kernels, pack(): pl.pallas_call(pack_kernel, out_shape=(jax.ShapeDtypeStruct((clusters //...  2.36 us
    ppermute x1, starting transfers between devices, body(): low_other = lax.ppermute(low, BOTH, owner_swap)  1.92 us
    pallas_call x3, Pallas kernels, vmem_call(): pl.pallas_call(kernel, out_shape=jax.ShapeDtypeStruct(shape, F32), in_spe...  1.89 us
  transfers between devices with their start and end apart: 5, of which 3 were waited for; matrix products, arithmetic and copies ran while one was open for 0% of the time, Pallas kernels for 4%

profile of v4, /device:TPU:1, one launch (start us, length us, event | category | flops | bytes accessed | tf_op | source)
XLA Modules:
  0.0 71.8 jit_solution(8751160485020064624)
XLA Ops:
  0.0 2.4 %pack.1 = (bf16[64,4,1024]{2,1,0:T(4,128)(2,1)S(1)}, s32[64,128]{1,0:T(8,128)S(1)}) custom-call(f32[256,1024]{1,0:T(8,128)} %emb_hbm.1, s32[1024,128]{1,0:T(8,128)} %bitcast.13, s32[1,128]{1,0:T(1,128)} %bitcast.14), custom_call_target="tpu_custom_call" | custom-call | tf_op jit(solution)/shard_map/pack/pallas_call | solution.py:140
  2.4 31.6 %all_to_all.16.direct_ref = bf16[64,4,1024]{2,1,0:T(4,128)(2,1)S(1)} all-to-all(bf16[64,4,1024]{2,1,0:T(4,128)(2,1)S(1)} %get-tuple-element.16), channel_id=1, replica_groups={{0,4,10,14,16,20,26,30,34,38,40,44,50,54,56,60,64,68,74,78,80,84,90,94,..., dimensions={0} | all-to-all | bytes 1048576 | tf_op jit(solution)/shard_map/all_to_all | solution.py:311
  34.0 3.5 %collective-permute-start.2 = (bf16[64,4,1024]{2,1,0:T(4,128)(2,1)S(1)}, bf16[64,4,1024]{2,1,0:T(4,128)(2,1)S(1)}, u32[]{:S(2)}, u32[]{:S(2)}) collective-permute-start(bf16[64,4,1024]{2,1,0:T(4,128)(2,1)S(1)} %all_to_all.16.direct_ref), channel_id=1, source_target_pairs={{0,1},{1,0},{2,3},{3,2},{4,5},{5,4},{6,7},{7,6},{8,9},{9,8},{10,11... | collective-permute-start | bytes 1572872 | tf_op jit(solution)/shard_map/ppermute | solution.py:318
  37.5 0.1 slice.9
  37.6 1.3 %collective-permute-start.1 = (bf16[40,4,1024]{2,1,0:T(4,128)(2,1)S(1)}, bf16[40,4,1024]{2,1,0:T(4,128)(2,1)S(1)}, u32[]{:S(2)}, u32[]{:S(2)}) collective-permute-start(bf16[40,4,1024]{2,1,0:T(4,128)(2,1)S(1)} %slice.9), channel_id=1, source_target_pairs={{24,0},{28,4},{18,10},{22,14},{8,16},{12,20},{2,26},{6,30},{58,34}... | collective-permute-start | bytes 983048 | tf_op jit(solution)/shard_map/ppermute | solution.py:314
  38.9 0.1 slice.8
  39.0 1.3 %collective-permute-start = (bf16[24,4,1024]{2,1,0:T(4,128)(2,1)S(1)}, bf16[24,4,1024]{2,1,0:T(4,128)(2,1)S(1)}, u32[]{:S(2)}, u32[]{:S(2)}) collective-permute-start(bf16[24,4,1024]{2,1,0:T(4,128)(2,1)S(1)} %slice.8), channel_id=1, source_target_pairs={{8,0},{12,4},{2,10},{6,14},{24,16},{28,20},{18,26},{22,30},{42,34}... | collective-permute-start | bytes 589832 | tf_op jit(solution)/shard_map/ppermute | solution.py:315
  40.3 1.3 %labels.1 = (f32[8,512]{1,0:T(8,128)S(1)}, f32[1024,128]{1,0:T(8,128)S(1)}) custom-call(s32[128,2,512]{2,1,0:T(2,128)} %ids_hbm, s32[1,128]{1,0:T(1,128)} %bitcast.15), custom_call_target="tpu_custom_call" | custom-call | flops 1000000000 | bytes 4194304 | tf_op jit(solution)/shard_map/labels/pallas_call | solution.py:193
  41.6 0.0 collective-permute-done.2.direct_other_ref
  41.6 0.5 score_direct.1.best_direct_ref
  42.1 3.6 %collective-permute-done.low_ref = bf16[24,4,1024]{2,1,0:T(4,128)(2,1)S(1)} collective-permute-done((bf16[24,4,1024]{2,1,0:T(4,128)(2,1)S(1)}, bf16[24,4,1024]{2,1,0:T(4,128)(2,1)S(1)}, u32[]{:S(2)}, u32[]{:S(2)}) %collective-permute-start) | collective-permute-done | bytes 196640 | tf_op jit(solution)/shard_map/ppermute | solution.py:315
  45.7 1.2 %collective-permute-done.1.high_ref = bf16[40,4,1024]{2,1,0:T(4,128)(2,1)S(1)} collective-permute-done((bf16[40,4,1024]{2,1,0:T(4,128)(2,1)S(1)}, bf16[40,4,1024]{2,1,0:T(4,128)(2,1)S(1)}, u32[]{:S(2)}, u32[]{:S(2)}) %collective-permute-start.1) | collective-permute-done | bytes 327712 | tf_op jit(solution)/shard_map/ppermute | solution.py:314
  47.0 2.8 %collective-permute-start.4 = (bf16[40,4,1024]{2,1,0:T(4,128)(2,1)S(1)}, bf16[40,4,1024]{2,1,0:T(4,128)(2,1)S(1)}, u32[]{:S(2)}, u32[]{:S(2)}) collective-permute-start(bf16[40,4,1024]{2,1,0:T(4,128)(2,1)S(1)} %collective-permute-done.1.high_ref), channel_id=1, source_target_pairs={{0,1},{1,0},{4,5},{5,4},{10,11},{11,10},{14,15},{15,14},{16,17},{1... | collective-permute-start | bytes 983048 | tf_op jit(solution)/shard_map/ppermute | solution.py:324
  49.7 1.9 %collective-permute-start.3 = (bf16[24,4,1024]{2,1,0:T(4,128)(2,1)S(1)}, bf16[24,4,1024]{2,1,0:T(4,128)(2,1)S(1)}, u32[]{:S(2)}, u32[]{:S(2)}) collective-permute-start(bf16[24,4,1024]{2,1,0:T(4,128)(2,1)S(1)} %collective-permute-done.low_ref), channel_id=1, source_target_pairs={{0,1},{1,0},{4,5},{5,4},{10,11},{11,10},{14,15},{15,14},{16,17},{1... | collective-permute-start | bytes 589832 | tf_op jit(solution)/shard_map/ppermute | solution.py:323
  51.7 0.8 %score_passed.1.best_ref = f32[8,512]{1,0:T(8,128)S(1)} custom-call(f32[8,512]{1,0:T(8,128)S(1)} %get-tuple-element.19.row_ref, f32[1024,128]{1,0:T(8,128)S(1)} %get-tuple-element.20.col_ref, bf16[64,4,1024]{2,1,0:T(4,128)(2,1)S(1)} %all_to_all.16.direct_ref, bf16[64,4,1024]{2,1,0:T(4,128)(2,1)S(1)} %collective-permute-done.2.direct_other_ref, ...), custom_call_target="tpu_custom_call" | custom-call | flops 1000000000 | bytes 2097152 | tf_op jit(solution)/shard_map/score_passed/pallas_call | solution.py:268
  52.4 0.6 collective-permute-done.3.low_other_ref
  53.1 0.0 collective-permute-done.4.high_other_ref
  53.1 0.6 score_final.1
  53.7 17.4 %all_to_all.17 = f32[128,1,4]{2,1,0:T(1,128)S(1)} all-to-all(f32[128,1,4]{2,1,0:T(1,128)S(1)} %bitcast.12), channel_id=1, replica_groups={{0,4,10,14,16,20,26,30,34,38,40,44,50,54,56,60,64,68,74,78,80,84,90,94,..., dimensions={0} | all-to-all | bytes 4096 | tf_op jit(solution)/shard_map/all_to_all | solution.py:333
  71.1 0.7 unpack.1
Async XLA Ops:
  34.0 7.6 %collective-permute-start.2 = (bf16[64,4,1024]{2,1,0:T(4,128)(2,1)S(1)}, bf16[64,4,1024]{2,1,0:T(4,128)(2,1)S(1)}, u32[]{:S(2)}, u32[]{:S(2)}) collective-permute-start(bf16[64,4,1024]{2,1,0:T(4,128)(2,1)S(1)} %all_to_all.16.direct_ref), channel_id=1, source_target_pairs={{0,1},{1,0},{2,3},{3,2},{4,5},{5,4},{6,7},{7,6},{8,9},{9,8},{10,11... | collective-permute-start | bytes 1572872 | tf_op jit(solution)/shard_map/ppermute | solution.py:318
  37.6 9.3 %collective-permute-start.1 = (bf16[40,4,1024]{2,1,0:T(4,128)(2,1)S(1)}, bf16[40,4,1024]{2,1,0:T(4,128)(2,1)S(1)}, u32[]{:S(2)}, u32[]{:S(2)}) collective-permute-start(bf16[40,4,1024]{2,1,0:T(4,128)(2,1)S(1)} %slice.9), channel_id=1, source_target_pairs={{24,0},{28,4},{18,10},{22,14},{8,16},{12,20},{2,26},{6,30},{58,34}... | collective-permute-start | bytes 983048 | tf_op jit(solution)/shard_map/ppermute | solution.py:314
  39.0 6.7 %collective-permute-start = (bf16[24,4,1024]{2,1,0:T(4,128)(2,1)S(1)}, bf16[24,4,1024]{2,1,0:T(4,128)(2,1)S(1)}, u32[]{:S(2)}, u32[]{:S(2)}) collective-permute-start(bf16[24,4,1024]{2,1,0:T(4,128)(2,1)S(1)} %slice.8), channel_id=1, source_target_pairs={{8,0},{12,4},{2,10},{6,14},{24,16},{28,20},{18,26},{22,30},{42,34}... | collective-permute-start | bytes 589832 | tf_op jit(solution)/shard_map/ppermute | solution.py:315
  47.0 6.1 %collective-permute-start.4 = (bf16[40,4,1024]{2,1,0:T(4,128)(2,1)S(1)}, bf16[40,4,1024]{2,1,0:T(4,128)(2,1)S(1)}, u32[]{:S(2)}, u32[]{:S(2)}) collective-permute-start(bf16[40,4,1024]{2,1,0:T(4,128)(2,1)S(1)} %collective-permute-done.1.high_ref), channel_id=1, source_target_pairs={{0,1},{1,0},{4,5},{5,4},{10,11},{11,10},{14,15},{15,14},{16,17},{1... | collective-permute-start | bytes 983048 | tf_op jit(solution)/shard_map/ppermute | solution.py:324
  49.7 3.3 %collective-permute-start.3 = (bf16[24,4,1024]{2,1,0:T(4,128)(2,1)S(1)}, bf16[24,4,1024]{2,1,0:T(4,128)(2,1)S(1)}, u32[]{:S(2)}, u32[]{:S(2)}) collective-permute-start(bf16[24,4,1024]{2,1,0:T(4,128)(2,1)S(1)} %collective-permute-done.low_ref), channel_id=1, source_target_pairs={{0,1},{1,0},{4,5},{5,4},{10,11},{11,10},{14,15},{15,14},{16,17},{1... | collective-permute-start | bytes 589832 | tf_op jit(solution)/shard_map/ppermute | solution.py:323

commit v5 on v4

--- a/solution.py
+++ b/solution.py
@@ -290,22 +290,22 @@
 def chip_routes():
     owners = [owner_chip(position) for position in range(64)]
     direct, passing, back = [], [], []
-    low, high = [], []
+    low, high, swap = [], [], []
     for core in range(2):
         near, far = (4, 12) if core == 0 else (1, 3)
         direct.append([chip * 2 + core for chip in owners])
         passing.append([(chip ^ near) * 2 + core for chip in owners])
         back.append(direct[-1] + passing[-1])
-        low += [((chip ^ near) * 2 + core, chip * 2 + core) for chip in owners]
-        high += [((chip ^ far) * 2 + core, chip * 2 + core) for chip in owners]
-    swap = [(device, device ^ 1) for device in range(256)]
-    owner_swap = [(device, device ^ 1) for device in range(256) if chip_parity(device // 2) == 0]
-    return direct + passing, back, low, high, swap, owner_swap
+        for chip in range(128):
+            low.append(((chip ^ near) * 2 + core, chip * 2 + core))
+            high.append(((chip ^ far) * 2 + core, chip * 2 + core))
+            swap.append((chip * 2 + core, chip * 2 + 1 - core))
+    return direct + passing, back, low, high, swap
 
 
 def body(embeddings, block_ids, block_counts):
     doc_rows = embeddings.shape[0]
-    send_groups, back_groups, low_route, high_route, swap, owner_swap = chip_routes()
+    send_groups, back_groups, low_route, high_route, swap = chip_routes()
     counts = block_counts.reshape(1, -1)
     packed, docs = pack(embeddings, block_ids, counts)
     direct = lax.all_to_all(
@@ -320,8 +320,8 @@
         direct_kernel, (8, 256), "score_direct", 10**9, row, col, direct, direct_other
     )
     low, high, best = lax.optimization_barrier((low, high, best))
-    low_other = lax.ppermute(low, BOTH, owner_swap)
-    high_other = lax.ppermute(high, BOTH, owner_swap)
+    low_other = lax.ppermute(low, BOTH, swap)
+    high_other = lax.ppermute(high, BOTH, swap)
     best = vmem_call(
         passed_kernel, (8, 512), "score_passed", 10**9,
         row, col, direct, direct_other, low, high, best,

time: 72.1 us -> 66.7 us (0.925)
  starting transfers between devices: 10.8 us -> 6.2 us
  waiting for transfers between devices: 5.51 us -> 4.64 us
    ppermute x2, starting transfers between devices: 4.68 us -> 0.86 us  [the longest x1 0.86 us: body(): high_other = lax.ppermute(high, BOTH, swap)]
    ppermute x1, starting transfers between devices: 1.29 us -> 0.09 us  [body(): low = lax.ppermute(direct[:LOW], BOTH, low_route)]
where the time goes in v5:
time: 66.7 us; the launch traced here: 66.5 us
  blocking collectives  49.2 us (74%)
  Pallas kernels  6.22 us (9%)
  starting transfers between devices  6.2 us (9%)
  waiting for transfers between devices  4.64 us (7%)
    all_to_all x1, blocking collectives, body(): lax.all_to_all(packed, BOTH, split_axis=0, concat_axis=0, axis_index_grou...  31.6 us
    all_to_all x1, blocking collectives, body(): lax.all_to_all(best, BOTH, split_axis=0, concat_axis=0, axis_index_groups...  17.6 us
    ppermute x1, starting transfers between devices, body(): direct_other = lax.ppermute(direct, BOTH, swap)  3.55 us
    ppermute x1, waiting for transfers between devices, body(): low = lax.ppermute(direct[:LOW], BOTH, low_route)  3.03 us
    pallas_call x1, Pallas kernels, pack(): pl.pallas_call(pack_kernel, out_shape=(jax.ShapeDtypeStruct((clusters //...  2.36 us
    pallas_call x3, Pallas kernels, vmem_call(): pl.pallas_call(kernel, out_shape=jax.ShapeDtypeStruct(shape, F32), in_spe...  1.88 us
    ppermute x1, starting transfers between devices, body(): high = lax.ppermute(direct[LOW:], BOTH, high_route)  1.7 us
  transfers between devices with their start and end apart: 5, of which 3 were waited for; matrix products, arithmetic and copies ran while one was open for 0% of the time, Pallas kernels for 4%

profile of v5, /device:TPU:1, one launch (start us, length us, event | category | flops | bytes accessed | tf_op | source)
XLA Modules:
  0.0 66.5 jit_solution(907741574937574788)
XLA Ops:
  0.0 2.4 %pack.1 = (bf16[64,4,1024]{2,1,0:T(4,128)(2,1)S(1)}, s32[64,128]{1,0:T(8,128)S(1)}) custom-call(f32[256,1024]{1,0:T(8,128)} %emb_hbm.1, s32[1024,128]{1,0:T(8,128)} %bitcast.13, s32[1,128]{1,0:T(1,128)} %bitcast.14), custom_call_target="tpu_custom_call" | custom-call | tf_op jit(solution)/shard_map/pack/pallas_call | solution.py:140
  2.4 31.6 %all_to_all.16.direct_ref = bf16[64,4,1024]{2,1,0:T(4,128)(2,1)S(1)} all-to-all(bf16[64,4,1024]{2,1,0:T(4,128)(2,1)S(1)} %get-tuple-element.16), channel_id=1, replica_groups={{0,4,10,14,16,20,26,30,34,38,40,44,50,54,56,60,64,68,74,78,80,84,90,94,..., dimensions={0} | all-to-all | bytes 1048576 | tf_op jit(solution)/shard_map/all_to_all | solution.py:311
  34.0 3.5 %collective-permute-start.2 = (bf16[64,4,1024]{2,1,0:T(4,128)(2,1)S(1)}, bf16[64,4,1024]{2,1,0:T(4,128)(2,1)S(1)}, u32[]{:S(2)}, u32[]{:S(2)}) collective-permute-start(bf16[64,4,1024]{2,1,0:T(4,128)(2,1)S(1)} %all_to_all.16.direct_ref), channel_id=1, source_target_pairs={{0,1},{2,3},{4,5},{6,7},{8,9},{10,11},{12,13},{14,15},{16,17},{18,... | collective-permute-start | bytes 1572872 | tf_op jit(solution)/shard_map/ppermute | solution.py:318
  37.5 0.1 slice.9
  37.6 1.7 %collective-permute-start.1 = (bf16[40,4,1024]{2,1,0:T(4,128)(2,1)S(1)}, bf16[40,4,1024]{2,1,0:T(4,128)(2,1)S(1)}, u32[]{:S(2)}, u32[]{:S(2)}) collective-permute-start(bf16[40,4,1024]{2,1,0:T(4,128)(2,1)S(1)} %slice.9), channel_id=1, source_target_pairs={{24,0},{26,2},{28,4},{30,6},{16,8},{18,10},{20,12},{22,14},{8,16},... | collective-permute-start | bytes 983048 | tf_op jit(solution)/shard_map/ppermute | solution.py:314
  39.3 0.1 slice.8
  39.4 0.1 collective-permute-start
  39.5 1.3 %labels.1 = (f32[8,512]{1,0:T(8,128)S(1)}, f32[1024,128]{1,0:T(8,128)S(1)}) custom-call(s32[128,2,512]{2,1,0:T(2,128)} %ids_hbm, s32[1,128]{1,0:T(1,128)} %bitcast.15), custom_call_target="tpu_custom_call" | custom-call | flops 1000000000 | bytes 4194304 | tf_op jit(solution)/shard_map/labels/pallas_call | solution.py:193
  40.8 0.0 collective-permute-done.2.direct_other_ref
  40.8 0.5 score_direct.1.best_direct_ref
  41.3 3.0 %collective-permute-done.low_ref = bf16[24,4,1024]{2,1,0:T(4,128)(2,1)S(1)} collective-permute-done((bf16[24,4,1024]{2,1,0:T(4,128)(2,1)S(1)}, bf16[24,4,1024]{2,1,0:T(4,128)(2,1)S(1)}, u32[]{:S(2)}, u32[]{:S(2)}) %collective-permute-start) | collective-permute-done | bytes 196640 | tf_op jit(solution)/shard_map/ppermute | solution.py:315
  44.3 0.8 %collective-permute-done.1.high_ref = bf16[40,4,1024]{2,1,0:T(4,128)(2,1)S(1)} collective-permute-done((bf16[40,4,1024]{2,1,0:T(4,128)(2,1)S(1)}, bf16[40,4,1024]{2,1,0:T(4,128)(2,1)S(1)}, u32[]{:S(2)}, u32[]{:S(2)}) %collective-permute-start.1) | collective-permute-done | bytes 327712 | tf_op jit(solution)/shard_map/ppermute | solution.py:314
  45.2 0.9 %collective-permute-start.4 = (bf16[40,4,1024]{2,1,0:T(4,128)(2,1)S(1)}, bf16[40,4,1024]{2,1,0:T(4,128)(2,1)S(1)}, u32[]{:S(2)}, u32[]{:S(2)}) collective-permute-start(bf16[40,4,1024]{2,1,0:T(4,128)(2,1)S(1)} %collective-permute-done.1.high_ref), channel_id=1, source_target_pairs={{0,1},{2,3},{4,5},{6,7},{8,9},{10,11},{12,13},{14,15},{16,17},{18,... | collective-permute-start | bytes 983048 | tf_op jit(solution)/shard_map/ppermute | solution.py:324
  46.0 0.0 collective-permute-start.3
  46.0 0.8 %score_passed.1.best_ref = f32[8,512]{1,0:T(8,128)S(1)} custom-call(f32[8,512]{1,0:T(8,128)S(1)} %get-tuple-element.19.row_ref, f32[1024,128]{1,0:T(8,128)S(1)} %get-tuple-element.20.col_ref, bf16[64,4,1024]{2,1,0:T(4,128)(2,1)S(1)} %all_to_all.16.direct_ref, bf16[64,4,1024]{2,1,0:T(4,128)(2,1)S(1)} %collective-permute-done.2.direct_other_ref, ...), custom_call_target="tpu_custom_call" | custom-call | flops 1000000000 | bytes 2097152 | tf_op jit(solution)/shard_map/score_passed/pallas_call | solution.py:268
  46.8 0.8 %collective-permute-done.3.low_other_ref = bf16[24,4,1024]{2,1,0:T(4,128)(2,1)S(1)} collective-permute-done((bf16[24,4,1024]{2,1,0:T(4,128)(2,1)S(1)}, bf16[24,4,1024]{2,1,0:T(4,128)(2,1)S(1)}, u32[]{:S(2)}, u32[]{:S(2)}) %collective-permute-start.3) | collective-permute-done | bytes 196640 | tf_op jit(solution)/shard_map/ppermute | solution.py:323
  47.6 0.0 collective-permute-done.4.high_other_ref
  47.6 0.6 score_final.1
  48.2 17.6 %all_to_all.17 = f32[128,1,4]{2,1,0:T(1,128)S(1)} all-to-all(f32[128,1,4]{2,1,0:T(1,128)S(1)} %bitcast.12), channel_id=1, replica_groups={{0,4,10,14,16,20,26,30,34,38,40,44,50,54,56,60,64,68,74,78,80,84,90,94,..., dimensions={0} | all-to-all | bytes 4096 | tf_op jit(solution)/shard_map/all_to_all | solution.py:333
  65.8 0.7 %unpack.1 = f32[1,256]{1,0:T(1,128)} custom-call(s32[64,128]{1,0:T(8,128)S(1)} %get-tuple-element.15.doc_ref, f32[128,4]{1,0:T(8,128)S(1)} %bitcast.11), custom_call_target="tpu_custom_call" | custom-call | tf_op jit(solution)/shard_map/unpack/pallas_call | solution.py:336
Async XLA Ops:
  34.0 6.8 %collective-permute-start.2 = (bf16[64,4,1024]{2,1,0:T(4,128)(2,1)S(1)}, bf16[64,4,1024]{2,1,0:T(4,128)(2,1)S(1)}, u32[]{:S(2)}, u32[]{:S(2)}) collective-permute-start(bf16[64,4,1024]{2,1,0:T(4,128)(2,1)S(1)} %all_to_all.16.direct_ref), channel_id=1, source_target_pairs={{0,1},{2,3},{4,5},{6,7},{8,9},{10,11},{12,13},{14,15},{16,17},{18,... | collective-permute-start | bytes 1572872 | tf_op jit(solution)/shard_map/ppermute | solution.py:318
  37.6 7.5 %collective-permute-start.1 = (bf16[40,4,1024]{2,1,0:T(4,128)(2,1)S(1)}, bf16[40,4,1024]{2,1,0:T(4,128)(2,1)S(1)}, u32[]{:S(2)}, u32[]{:S(2)}) collective-permute-start(bf16[40,4,1024]{2,1,0:T(4,128)(2,1)S(1)} %slice.9), channel_id=1, source_target_pairs={{24,0},{26,2},{28,4},{30,6},{16,8},{18,10},{20,12},{22,14},{8,16},... | collective-permute-start | bytes 983048 | tf_op jit(solution)/shard_map/ppermute | solution.py:314
  39.4 4.9 %collective-permute-start = (bf16[24,4,1024]{2,1,0:T(4,128)(2,1)S(1)}, bf16[24,4,1024]{2,1,0:T(4,128)(2,1)S(1)}, u32[]{:S(2)}, u32[]{:S(2)}) collective-permute-start(bf16[24,4,1024]{2,1,0:T(4,128)(2,1)S(1)} %slice.8), channel_id=1, source_target_pairs={{8,0},{10,2},{12,4},{14,6},{0,8},{2,10},{4,12},{6,14},{24,16},{26,... | collective-permute-start | bytes 589832 | tf_op jit(solution)/shard_map/ppermute | solution.py:315
  45.2 2.4 %collective-permute-start.4 = (bf16[40,4,1024]{2,1,0:T(4,128)(2,1)S(1)}, bf16[40,4,1024]{2,1,0:T(4,128)(2,1)S(1)}, u32[]{:S(2)}, u32[]{:S(2)}) collective-permute-start(bf16[40,4,1024]{2,1,0:T(4,128)(2,1)S(1)} %collective-permute-done.1.high_ref), channel_id=1, source_target_pairs={{0,1},{2,3},{4,5},{6,7},{8,9},{10,11},{12,13},{14,15},{16,17},{18,... | collective-permute-start | bytes 983048 | tf_op jit(solution)/shard_map/ppermute | solution.py:324
  46.0 1.5 %collective-permute-start.3 = (bf16[24,4,1024]{2,1,0:T(4,128)(2,1)S(1)}, bf16[24,4,1024]{2,1,0:T(4,128)(2,1)S(1)}, u32[]{:S(2)}, u32[]{:S(2)}) collective-permute-start(bf16[24,4,1024]{2,1,0:T(4,128)(2,1)S(1)} %collective-permute-done.low_ref), channel_id=1, source_target_pairs={{0,1},{2,3},{4,5},{6,7},{8,9},{10,11},{12,13},{14,15},{16,17},{18,... | collective-permute-start | bytes 589832 | tf_op jit(solution)/shard_map/ppermute | solution.py:323

commit v6 on v3

--- a/solution.py
+++ b/solution.py
@@ -12,7 +12,8 @@
 I32 = jnp.int32
 MIB = 1024 * 1024
 BOTH = ("dp", "pair")
-LOW = 24
+FIRST = 37
+LOW = 28
 
 
 def iota(shape, dim):
@@ -33,6 +34,10 @@
 
 def chip_position(chip):
     return chip >> 1
+
+
+def listed(place):
+    return (place + FIRST) & 63
 
 
 def owner_chip(position):
@@ -68,7 +73,8 @@
     doc_total = doc_rows * 2 * clusters
     chip, core = my_place()
     first = (chip * 2 + core) * doc_rows
-    turned = (chip_parity(chip) == 1) & (chip_position(chip) >= LOW)
+    near_pair = chip_position(chip) ^ jnp.where(core == 0, 2, 0)
+    turned = (chip_parity(chip) == 1) & (((near_pair - FIRST) & 63) >= LOW)
     flip = jnp.where(turned, jnp.where(core == 0, 4, 1), 0)
     diagonal = iota((clusters, clusters), 0) == iota((clusters, clusters), 1)
     even = iota((clusters, 1), 0) % 2 == 0
@@ -109,14 +115,14 @@
     pairs = clusters // 2
     rows = 4 * pairs
     row, spot = iota((rows, 4 * clusters), 0), iota((rows, 4 * clusters), 1)
-    spread = (spot == (row & 3) * clusters + 2 * ((row >> 2) ^ flip)).astype(BF16)
+    spread = (spot == (row & 3) * clusters + 2 * (listed(row >> 2) ^ flip)).astype(BF16)
     last = (((1,), (1,)), ((), ()))
     pick = lax.dot_general(
         spread, jnp.concatenate(hits, axis=1), last, preferred_element_type=F32
     ).astype(BF16)
-    take_pair = (iota((pairs, clusters), 1) == 2 * iota((pairs, clusters), 0)).astype(BF16)
+    take_pair = iota((pairs, clusters), 1) == 2 * listed(iota((pairs, clusters), 0))
     doc_ref[...] = lax.dot_general(
-        take_pair, picked.astype(BF16), last, preferred_element_type=F32
+        take_pair.astype(BF16), picked.astype(BF16), last, preferred_element_type=F32
     ).astype(I32)
     copies[2].wait()
     emb = emb_ref[...]
@@ -167,7 +173,7 @@
     group = iota((256, 1), 0)
     of_core = jnp.where(group < 128, core, 1 - core)
     hop = jnp.where(of_core == 0, 4, 1)
-    base = owner_chip(group & 63)
+    base = owner_chip(listed(group & 63))
     source = jnp.where((group & 64) == 0, base, base ^ hop) * 2 + of_core
     counts_copy.wait()
     counts = counts_ref[...]
@@ -283,24 +289,24 @@
 
 
 def chip_routes():
-    owners = [owner_chip(position) for position in range(64)]
+    owners = [owner_chip(listed(place)) for place in range(64)]
     direct, passing, back = [], [], []
-    low, high = [], []
+    low, high, swap = [], [], []
     for core in range(2):
         near, far = (4, 12) if core == 0 else (1, 3)
         direct.append([chip * 2 + core for chip in owners])
         passing.append([(chip ^ near) * 2 + core for chip in owners])
         back.append(direct[-1] + passing[-1])
-        low += [((chip ^ near) * 2 + core, chip * 2 + core) for chip in owners]
-        high += [((chip ^ far) * 2 + core, chip * 2 + core) for chip in owners]
-    swap = [(device, device ^ 1) for device in range(256)]
-    owner_swap = [(device, device ^ 1) for device in range(256) if chip_parity(device // 2) == 0]
-    return direct + passing, back, low, high, swap, owner_swap
+        for chip in range(128):
+            low.append(((chip ^ near) * 2 + core, chip * 2 + core))
+            high.append(((chip ^ far) * 2 + core, chip * 2 + core))
+            swap.append((chip * 2 + core, chip * 2 + 1 - core))
+    return direct + passing, back, low, high, swap
 
 
 def body(embeddings, block_ids, block_counts):
     doc_rows = embeddings.shape[0]
-    send_groups, back_groups, low_route, high_route, swap, owner_swap = chip_routes()
+    send_groups, back_groups, low_route, high_route, swap = chip_routes()
     counts = block_counts.reshape(1, -1)
     packed, docs = pack(embeddings, block_ids, counts)
     direct = lax.all_to_all(
@@ -312,10 +318,10 @@
     row, col = labels(late_ids, late_counts)
     direct_other = lax.ppermute(direct, BOTH, swap)
     best = vmem_call(direct_kernel, (8, 256), "score_direct", 10**9, row, col, direct)
+    low, best = lax.optimization_barrier((low, best))
+    low_other = lax.ppermute(low, BOTH, swap)
     high, best = lax.optimization_barrier((high, best))
-    high_other = lax.ppermute(high, BOTH, owner_swap)
-    low, best = lax.optimization_barrier((low, best))
-    low_other = lax.ppermute(low, BOTH, owner_swap)
+    high_other = lax.ppermute(high, BOTH, swap)
     best = vmem_call(
         passed_kernel, (8, 512), "score_passed", 10**9,
         row, col, direct, direct_other, low, high, best,

time: 72.1 us -> 60.2 us (0.83)
  starting transfers between devices: 14.7 us -> 7.1 us
  blocking collectives: 49 us -> 42 us
  waiting for transfers between devices: 1.58 us -> 4.15 us
    ppermute x2, starting transfers between devices: 8.52 us -> 1.68 us  [the longest x1 1.68 us: body(): high_other = lax.ppermute(high, BOTH, swap)]
    all_to_all x1, blocking collectives: 31.6 us -> 27.3 us  [body(): lax.all_to_all(packed, BOTH, split_axis=0, concat_axis=0, axis_index_grou...]
    ppermute x1, waiting for transfers between devices: 0.01 us -> 3.52 us  [body(): low = lax.ppermute(direct[:LOW], BOTH, low_route)]
    all_to_all x1, blocking collectives: 17.4 us -> 14.7 us  [body(): lax.all_to_all(best, BOTH, split_axis=0, concat_axis=0, axis_index_groups...]
    ppermute x1, starting transfers between devices: 1.29 us -> 3.28 us  [body(): high = lax.ppermute(direct[LOW:], BOTH, high_route)]
    ppermute x1, starting transfers between devices: 3.64 us -> 2.05 us  [body(): direct_other = lax.ppermute(direct, BOTH, swap)]
    ppermute x1, starting transfers between devices: 1.29 us -> 0.09 us  [body(): low = lax.ppermute(direct[:LOW], BOTH, low_route)]
    ppermute x1, waiting for transfers between devices: 1.09 us -> 0.01 us  [body(): high = lax.ppermute(direct[LOW:], BOTH, high_route)]
where the time goes in v6:
time: 60.2 us; the launch traced here: 59.7 us
  blocking collectives  42 us (70%)
  starting transfers between devices  7.1 us (12%)
  Pallas kernels  6.23 us (10%)
  waiting for transfers between devices  4.15 us (7%)
    all_to_all x1, blocking collectives, body(): lax.all_to_all(packed, BOTH, split_axis=0, concat_axis=0, axis_index_grou...  27.3 us
    all_to_all x1, blocking collectives, body(): lax.all_to_all(best, BOTH, split_axis=0, concat_axis=0, axis_index_groups...  14.7 us
    ppermute x1, waiting for transfers between devices, body(): low = lax.ppermute(direct[:LOW], BOTH, low_route)  3.52 us
    ppermute x1, starting transfers between devices, body(): high = lax.ppermute(direct[LOW:], BOTH, high_route)  3.28 us
    pallas_call x1, Pallas kernels, pack(): pl.pallas_call(pack_kernel, out_shape=(jax.ShapeDtypeStruct((clusters //...  2.36 us
    ppermute x1, starting transfers between devices, body(): direct_other = lax.ppermute(direct, BOTH, swap)  2.05 us
    pallas_call x3, Pallas kernels, vmem_call(): pl.pallas_call(kernel, out_shape=jax.ShapeDtypeStruct(shape, F32), in_spe...  1.89 us
    ppermute x1, starting transfers between devices, body(): high_other = lax.ppermute(high, BOTH, swap)  1.68 us
  transfers between devices with their start and end apart: 5, of which 2 were waited for; matrix products, arithmetic and copies ran while one was open for 0% of the time, Pallas kernels for 4%

profile of v6, /device:TPU:1, one launch (start us, length us, event | category | flops | bytes accessed | tf_op | source)
XLA Modules:
  0.0 59.7 jit_solution(3489559877235825107)
XLA Ops:
  0.0 2.4 %pack.1 = (bf16[64,4,1024]{2,1,0:T(4,128)(2,1)S(1)}, s32[64,128]{1,0:T(8,128)S(1)}) custom-call(f32[256,1024]{1,0:T(8,128)} %emb_hbm.1, s32[1024,128]{1,0:T(8,128)} %bitcast.13, s32[1,128]{1,0:T(1,128)} %bitcast.14), custom_call_target="tpu_custom_call" | custom-call | tf_op jit(solution)/shard_map/pack/pallas_call | solution.py:146
  2.4 27.3 %all_to_all.16.direct_ref = bf16[64,4,1024]{2,1,0:T(4,128)(2,1)S(1)} all-to-all(bf16[64,4,1024]{2,1,0:T(4,128)(2,1)S(1)} %get-tuple-element.17), channel_id=1, replica_groups={{148,154,158,162,166,168,172,178,182,184,188,192,196,202,206,208,212,21..., dimensions={0} | all-to-all | bytes 1048576 | tf_op jit(solution)/shard_map/all_to_all | solution.py:312
  29.7 2.1 %collective-permute-start.4 = (bf16[64,4,1024]{2,1,0:T(4,128)(2,1)S(1)}, bf16[64,4,1024]{2,1,0:T(4,128)(2,1)S(1)}, u32[]{:S(2)}, u32[]{:S(2)}) collective-permute-start(bf16[64,4,1024]{2,1,0:T(4,128)(2,1)S(1)} %all_to_all.16.direct_ref), channel_id=1, source_target_pairs={{0,1},{2,3},{4,5},{6,7},{8,9},{10,11},{12,13},{14,15},{16,17},{18,... | collective-permute-start | bytes 1572872 | tf_op jit(solution)/shard_map/ppermute | solution.py:319
  31.7 0.1 slice.9
  31.9 3.3 %collective-permute-start.1 = (bf16[36,4,1024]{2,1,0:T(4,128)(2,1)S(1)}, bf16[36,4,1024]{2,1,0:T(4,128)(2,1)S(1)}, u32[]{:S(2)}, u32[]{:S(2)}) collective-permute-start(bf16[36,4,1024]{2,1,0:T(4,128)(2,1)S(1)} %slice.9), channel_id=1, source_target_pairs={{24,0},{26,2},{28,4},{30,6},{16,8},{18,10},{20,12},{22,14},{8,16},... | collective-permute-start | bytes 884744 | tf_op jit(solution)/shard_map/ppermute | solution.py:315
  35.1 0.1 slice.8
  35.2 0.1 collective-permute-start
  35.3 1.3 %labels.1 = (f32[8,512]{1,0:T(8,128)S(1)}, f32[1024,128]{1,0:T(8,128)S(1)}) custom-call(s32[128,2,512]{2,1,0:T(2,128)} %ids_hbm, s32[1,128]{1,0:T(1,128)} %bitcast.15), custom_call_target="tpu_custom_call" | custom-call | flops 1000000000 | bytes 4194304 | tf_op jit(solution)/shard_map/labels/pallas_call | solution.py:199
  36.6 0.3 score_direct.1.best_direct_ref
  36.9 3.5 %collective-permute-done.low_ref = bf16[28,4,1024]{2,1,0:T(4,128)(2,1)S(1)} collective-permute-done((bf16[28,4,1024]{2,1,0:T(4,128)(2,1)S(1)}, bf16[28,4,1024]{2,1,0:T(4,128)(2,1)S(1)}, u32[]{:S(2)}, u32[]{:S(2)}) %collective-permute-start) | collective-permute-done | bytes 229408 | tf_op jit(solution)/shard_map/ppermute | solution.py:316
  40.5 0.0 collective-permute-done.1.high_ref
  40.5 1.7 %collective-permute-start.3 = (bf16[36,4,1024]{2,1,0:T(4,128)(2,1)S(1)}, bf16[36,4,1024]{2,1,0:T(4,128)(2,1)S(1)}, u32[]{:S(2)}, u32[]{:S(2)}) collective-permute-start(bf16[36,4,1024]{2,1,0:T(4,128)(2,1)S(1)} %collective-permute-done.1.high_ref), channel_id=1, source_target_pairs={{0,1},{2,3},{4,5},{6,7},{8,9},{10,11},{12,13},{14,15},{16,17},{18,... | collective-permute-start | bytes 884744 | tf_op jit(solution)/shard_map/ppermute | solution.py:324
  42.2 0.0 collective-permute-start.2
  42.2 0.0 collective-permute-done.4.direct_other_ref
  42.2 0.9 %score_passed.1.best_ref = f32[8,512]{1,0:T(8,128)S(1)} custom-call(f32[8,512]{1,0:T(8,128)S(1)} %get-tuple-element.20.row_ref, f32[1024,128]{1,0:T(8,128)S(1)} %get-tuple-element.21.col_ref, bf16[64,4,1024]{2,1,0:T(4,128)(2,1)S(1)} %all_to_all.16.direct_ref, bf16[64,4,1024]{2,1,0:T(4,128)(2,1)S(1)} %collective-permute-done.4.direct_other_ref, ...), custom_call_target="tpu_custom_call" | custom-call | flops 1000000000 | bytes 2097152 | tf_op jit(solution)/shard_map/score_passed/pallas_call | solution.py:269
  43.1 0.6 %collective-permute-done.2.low_other_ref = bf16[28,4,1024]{2,1,0:T(4,128)(2,1)S(1)} collective-permute-done((bf16[28,4,1024]{2,1,0:T(4,128)(2,1)S(1)}, bf16[28,4,1024]{2,1,0:T(4,128)(2,1)S(1)}, u32[]{:S(2)}, u32[]{:S(2)}) %collective-permute-start.2) | collective-permute-done | bytes 229408 | tf_op jit(solution)/shard_map/ppermute | solution.py:322
  43.7 0.0 collective-permute-done.3.high_other_ref
  43.7 0.6 %score_final.1 = f32[128,4]{1,0:T(8,128)S(1)} custom-call(f32[8,512]{1,0:T(8,128)S(1)} %get-tuple-element.20.row_ref, f32[1024,128]{1,0:T(8,128)S(1)} %get-tuple-element.21.col_ref, bf16[64,4,1024]{2,1,0:T(4,128)(2,1)S(1)} %all_to_all.16.direct_ref, bf16[28,4,1024]{2,1,0:T(4,128)(2,1)S(1)} %collective-permute-done.low_ref, ...), custom_call_target="tpu_custom_call" | custom-call | flops 1000000000 | bytes 2097152 | tf_op jit(solution)/shard_map/score_final/pallas_call | solution.py:269
  44.3 14.7 %all_to_all.17 = f32[128,1,4]{2,1,0:T(1,128)S(1)} all-to-all(f32[128,1,4]{2,1,0:T(1,128)S(1)} %bitcast.12), channel_id=1, replica_groups={{148,154,158,162,166,168,172,178,182,184,188,192,196,202,206,208,212,21..., dimensions={0} | all-to-all | bytes 4096 | tf_op jit(solution)/shard_map/all_to_all | solution.py:333
  59.0 0.7 %unpack.1 = f32[1,256]{1,0:T(1,128)} custom-call(s32[64,128]{1,0:T(8,128)S(1)} %get-tuple-element.16.doc_ref, f32[128,4]{1,0:T(8,128)S(1)} %bitcast.11), custom_call_target="tpu_custom_call" | custom-call | tf_op jit(solution)/shard_map/unpack/pallas_call | solution.py:336
Async XLA Ops:
  29.7 12.5 %collective-permute-start.4 = (bf16[64,4,1024]{2,1,0:T(4,128)(2,1)S(1)}, bf16[64,4,1024]{2,1,0:T(4,128)(2,1)S(1)}, u32[]{:S(2)}, u32[]{:S(2)}) collective-permute-start(bf16[64,4,1024]{2,1,0:T(4,128)(2,1)S(1)} %all_to_all.16.direct_ref), channel_id=1, source_target_pairs={{0,1},{2,3},{4,5},{6,7},{8,9},{10,11},{12,13},{14,15},{16,17},{18,... | collective-permute-start | bytes 1572872 | tf_op jit(solution)/shard_map/ppermute | solution.py:319
  31.9 8.6 %collective-permute-start.1 = (bf16[36,4,1024]{2,1,0:T(4,128)(2,1)S(1)}, bf16[36,4,1024]{2,1,0:T(4,128)(2,1)S(1)}, u32[]{:S(2)}, u32[]{:S(2)}) collective-permute-start(bf16[36,4,1024]{2,1,0:T(4,128)(2,1)S(1)} %slice.9), channel_id=1, source_target_pairs={{24,0},{26,2},{28,4},{30,6},{16,8},{18,10},{20,12},{22,14},{8,16},... | collective-permute-start | bytes 884744 | tf_op jit(solution)/shard_map/ppermute | solution.py:315
  35.2 5.3 %collective-permute-start = (bf16[28,4,1024]{2,1,0:T(4,128)(2,1)S(1)}, bf16[28,4,1024]{2,1,0:T(4,128)(2,1)S(1)}, u32[]{:S(2)}, u32[]{:S(2)}) collective-permute-start(bf16[28,4,1024]{2,1,0:T(4,128)(2,1)S(1)} %slice.8), channel_id=1, source_target_pairs={{8,0},{10,2},{12,4},{14,6},{0,8},{2,10},{4,12},{6,14},{24,16},{26,... | collective-permute-start | bytes 688136 | tf_op jit(solution)/shard_map/ppermute | solution.py:316
  40.5 3.2 %collective-permute-start.3 = (bf16[36,4,1024]{2,1,0:T(4,128)(2,1)S(1)}, bf16[36,4,1024]{2,1,0:T(4,128)(2,1)S(1)}, u32[]{:S(2)}, u32[]{:S(2)}) collective-permute-start(bf16[36,4,1024]{2,1,0:T(4,128)(2,1)S(1)} %collective-permute-done.1.high_ref), channel_id=1, source_target_pairs={{0,1},{2,3},{4,5},{6,7},{8,9},{10,11},{12,13},{14,15},{16,17},{18,... | collective-permute-start | bytes 884744 | tf_op jit(solution)/shard_map/ppermute | solution.py:324
  42.2 1.5 %collective-permute-start.2 = (bf16[28,4,1024]{2,1,0:T(4,128)(2,1)S(1)}, bf16[28,4,1024]{2,1,0:T(4,128)(2,1)S(1)}, u32[]{:S(2)}, u32[]{:S(2)}) collective-permute-start(bf16[28,4,1024]{2,1,0:T(4,128)(2,1)S(1)} %collective-permute-done.low_ref), channel_id=1, source_target_pairs={{0,1},{2,3},{4,5},{6,7},{8,9},{10,11},{12,13},{14,15},{16,17},{18,... | collective-permute-start | bytes 688136 | tf_op jit(solution)/shard_map/ppermute | solution.py:322

commit v7 on v6

--- a/solution.py
+++ b/solution.py
@@ -13,7 +13,7 @@
 MIB = 1024 * 1024
 BOTH = ("dp", "pair")
 FIRST = 37
-LOW = 28
+LOW = 32
 
 
 def iota(shape, dim):
@@ -75,7 +75,7 @@
     first = (chip * 2 + core) * doc_rows
     near_pair = chip_position(chip) ^ jnp.where(core == 0, 2, 0)
     turned = (chip_parity(chip) == 1) & (((near_pair - FIRST) & 63) >= LOW)
-    flip = jnp.where(turned, jnp.where(core == 0, 4, 1), 0)
+    flip = jnp.where(turned, jnp.where(core == 0, 10, 1), 0)
     diagonal = iota((clusters, clusters), 0) == iota((clusters, clusters), 1)
     even = iota((clusters, 1), 0) % 2 == 0
     lift = jnp.where(even, doc_rows, 0)
@@ -293,7 +293,7 @@
     direct, passing, back = [], [], []
     low, high, swap = [], [], []
     for core in range(2):
-        near, far = (4, 12) if core == 0 else (1, 3)
+        near, far = (4, 16) if core == 0 else (1, 3)
         direct.append([chip * 2 + core for chip in owners])
         passing.append([(chip ^ near) * 2 + core for chip in owners])
         back.append(direct[-1] + passing[-1])

time: 60.2 us -> 59.1 us (0.982)
  starting transfers between devices: 7.1 us -> 6.04 us
    ppermute x1, waiting for transfers between devices: 3.52 us -> 0.77 us  [body(): low = lax.ppermute(direct[:LOW], BOTH, low_route)]
    ppermute x1, waiting for transfers between devices: 0.01 us -> 2.38 us  [body(): high = lax.ppermute(direct[LOW:], BOTH, high_route)]
    ppermute x1, starting transfers between devices: 0.09 us -> 1.72 us  [body(): low = lax.ppermute(direct[:LOW], BOTH, low_route)]
    ppermute x1, starting transfers between devices: 3.28 us -> 1.66 us  [body(): high = lax.ppermute(direct[LOW:], BOTH, high_route)]
    ppermute x1, starting transfers between devices: 1.68 us -> 0.6 us  [body(): high_other = lax.ppermute(high, BOTH, swap)]
  transfers between devices with their start and end apart: 5 -> 5, of which waited for: 2 -> 4; matrix products, arithmetic and copies ran while one was open for 0% -> 0% of each run, Pallas kernels for 4% -> 4%
where the time goes in v7:
time: 59.1 us; the launch traced here: 58.6 us
  blocking collectives  42.4 us (72%)
  Pallas kernels  6.23 us (11%)
  starting transfers between devices  6.04 us (10%)
  waiting for transfers between devices  3.76 us (6%)
    all_to_all x1, blocking collectives, body(): lax.all_to_all(packed, BOTH, split_axis=0, concat_axis=0, axis_index_grou...  27.3 us
    all_to_all x1, blocking collectives, body(): lax.all_to_all(best, BOTH, split_axis=0, concat_axis=0, axis_index_groups...  15.1 us
    ppermute x1, waiting for transfers between devices, body(): high = lax.ppermute(direct[LOW:], BOTH, high_route)  2.38 us
    pallas_call x1, Pallas kernels, pack(): pl.pallas_call(pack_kernel, out_shape=(jax.ShapeDtypeStruct((clusters //...  2.36 us
    ppermute x1, starting transfers between devices, body(): direct_other = lax.ppermute(direct, BOTH, swap)  2.05 us
    pallas_call x3, Pallas kernels, vmem_call(): pl.pallas_call(kernel, out_shape=jax.ShapeDtypeStruct(shape, F32), in_spe...  1.89 us
    ppermute x1, starting transfers between devices, body(): low = lax.ppermute(direct[:LOW], BOTH, low_route)  1.72 us
    ppermute x1, starting transfers between devices, body(): high = lax.ppermute(direct[LOW:], BOTH, high_route)  1.66 us
  transfers between devices with their start and end apart: 5, of which 4 were waited for; matrix products, arithmetic and copies ran while one was open for 0% of the time, Pallas kernels for 4%

profile of v7, /device:TPU:1, one launch (start us, length us, event | category | flops | bytes accessed | tf_op | source)
XLA Modules:
  0.0 58.6 jit_solution(3438418409719904774)
XLA Ops:
  0.0 2.4 %pack.1 = (bf16[64,4,1024]{2,1,0:T(4,128)(2,1)S(1)}, s32[64,128]{1,0:T(8,128)S(1)}) custom-call(f32[256,1024]{1,0:T(8,128)} %emb_hbm.1, s32[1024,128]{1,0:T(8,128)} %bitcast.13, s32[1,128]{1,0:T(1,128)} %bitcast.14), custom_call_target="tpu_custom_call" | custom-call | tf_op jit(solution)/shard_map/pack/pallas_call | solution.py:146
  2.4 27.3 %all_to_all.16.direct_ref = bf16[64,4,1024]{2,1,0:T(4,128)(2,1)S(1)} all-to-all(bf16[64,4,1024]{2,1,0:T(4,128)(2,1)S(1)} %get-tuple-element.17), channel_id=1, replica_groups={{148,154,158,162,166,168,172,178,182,184,188,192,196,202,206,208,212,21..., dimensions={0} | all-to-all | bytes 1048576 | tf_op jit(solution)/shard_map/all_to_all | solution.py:312
  29.7 2.1 %collective-permute-start.4 = (bf16[64,4,1024]{2,1,0:T(4,128)(2,1)S(1)}, bf16[64,4,1024]{2,1,0:T(4,128)(2,1)S(1)}, u32[]{:S(2)}, u32[]{:S(2)}) collective-permute-start(bf16[64,4,1024]{2,1,0:T(4,128)(2,1)S(1)} %all_to_all.16.direct_ref), channel_id=1, source_target_pairs={{0,1},{2,3},{4,5},{6,7},{8,9},{10,11},{12,13},{14,15},{16,17},{18,... | collective-permute-start | bytes 1572872 | tf_op jit(solution)/shard_map/ppermute | solution.py:319
  31.7 0.2 fusion
  31.9 1.7 %collective-permute-start = (bf16[32,4,1024]{2,1,0:T(4,128)(2,1)S(1)}, bf16[32,4,1024]{2,1,0:T(4,128)(2,1)S(1)}, u32[]{:S(2)}, u32[]{:S(2)}) collective-permute-start(bf16[32,4,1024]{2,1,0:T(4,128)(2,1)S(1)} %get-tuple-element.28), channel_id=1, source_target_pairs={{8,0},{10,2},{12,4},{14,6},{0,8},{2,10},{4,12},{6,14},{24,16},{26,... | collective-permute-start | bytes 786440 | tf_op jit(solution)/shard_map/ppermute | solution.py:316
  33.7 1.7 %collective-permute-start.1 = (bf16[32,4,1024]{2,1,0:T(4,128)(2,1)S(1)}, bf16[32,4,1024]{2,1,0:T(4,128)(2,1)S(1)}, u32[]{:S(2)}, u32[]{:S(2)}) collective-permute-start(bf16[32,4,1024]{2,1,0:T(4,128)(2,1)S(1)} %get-tuple-element.27), channel_id=1, source_target_pairs={{32,0},{34,2},{36,4},{38,6},{40,8},{42,10},{44,12},{46,14},{48,16}... | collective-permute-start | bytes 786440 | tf_op jit(solution)/shard_map/ppermute | solution.py:315
  35.3 1.3 %labels.1 = (f32[8,512]{1,0:T(8,128)S(1)}, f32[1024,128]{1,0:T(8,128)S(1)}) custom-call(s32[128,2,512]{2,1,0:T(2,128)} %ids_hbm, s32[1,128]{1,0:T(1,128)} %bitcast.15), custom_call_target="tpu_custom_call" | custom-call | flops 1000000000 | bytes 4194304 | tf_op jit(solution)/shard_map/labels/pallas_call | solution.py:199
  36.6 0.3 score_direct.1.best_direct_ref
  36.9 0.8 %collective-permute-done.low_ref = bf16[32,4,1024]{2,1,0:T(4,128)(2,1)S(1)} collective-permute-done((bf16[32,4,1024]{2,1,0:T(4,128)(2,1)S(1)}, bf16[32,4,1024]{2,1,0:T(4,128)(2,1)S(1)}, u32[]{:S(2)}, u32[]{:S(2)}) %collective-permute-start) | collective-permute-done | bytes 262176 | tf_op jit(solution)/shard_map/ppermute | solution.py:316
  37.7 2.4 %collective-permute-done.1.high_ref = bf16[32,4,1024]{2,1,0:T(4,128)(2,1)S(1)} collective-permute-done((bf16[32,4,1024]{2,1,0:T(4,128)(2,1)S(1)}, bf16[32,4,1024]{2,1,0:T(4,128)(2,1)S(1)}, u32[]{:S(2)}, u32[]{:S(2)}) %collective-permute-start.1) | collective-permute-done | bytes 262176 | tf_op jit(solution)/shard_map/ppermute | solution.py:315
  40.1 0.6 %collective-permute-start.3 = (bf16[32,4,1024]{2,1,0:T(4,128)(2,1)S(1)}, bf16[32,4,1024]{2,1,0:T(4,128)(2,1)S(1)}, u32[]{:S(2)}, u32[]{:S(2)}) collective-permute-start(bf16[32,4,1024]{2,1,0:T(4,128)(2,1)S(1)} %collective-permute-done.1.high_ref), channel_id=1, source_target_pairs={{0,1},{2,3},{4,5},{6,7},{8,9},{10,11},{12,13},{14,15},{16,17},{18,... | collective-permute-start | bytes 786440 | tf_op jit(solution)/shard_map/ppermute | solution.py:324
  40.7 0.0 collective-permute-start.2
  40.7 0.0 collective-permute-done.4.direct_other_ref
  40.7 0.9 %score_passed.1.best_ref = f32[8,512]{1,0:T(8,128)S(1)} custom-call(f32[8,512]{1,0:T(8,128)S(1)} %get-tuple-element.20.row_ref, f32[1024,128]{1,0:T(8,128)S(1)} %get-tuple-element.21.col_ref, bf16[64,4,1024]{2,1,0:T(4,128)(2,1)S(1)} %all_to_all.16.direct_ref, bf16[64,4,1024]{2,1,0:T(4,128)(2,1)S(1)} %collective-permute-done.4.direct_other_ref, ...), custom_call_target="tpu_custom_call" | custom-call | flops 1000000000 | bytes 2097152 | tf_op jit(solution)/shard_map/score_passed/pallas_call | solution.py:269
  41.6 0.2 collective-permute-done.3.high_other_ref
  41.9 0.4 collective-permute-done.2.low_other_ref
  42.2 0.6 %score_final.1 = f32[128,4]{1,0:T(8,128)S(1)} custom-call(f32[8,512]{1,0:T(8,128)S(1)} %get-tuple-element.20.row_ref, f32[1024,128]{1,0:T(8,128)S(1)} %get-tuple-element.21.col_ref, bf16[64,4,1024]{2,1,0:T(4,128)(2,1)S(1)} %all_to_all.16.direct_ref, bf16[32,4,1024]{2,1,0:T(4,128)(2,1)S(1)} %collective-permute-done.low_ref, ...), custom_call_target="tpu_custom_call" | custom-call | flops 1000000000 | bytes 2097152 | tf_op jit(solution)/shard_map/score_final/pallas_call | solution.py:269
  42.9 15.1 %all_to_all.17 = f32[128,1,4]{2,1,0:T(1,128)S(1)} all-to-all(f32[128,1,4]{2,1,0:T(1,128)S(1)} %bitcast.12), channel_id=1, replica_groups={{148,154,158,162,166,168,172,178,182,184,188,192,196,202,206,208,212,21..., dimensions={0} | all-to-all | bytes 4096 | tf_op jit(solution)/shard_map/all_to_all | solution.py:333
  57.9 0.7 %unpack.1 = f32[1,256]{1,0:T(1,128)} custom-call(s32[64,128]{1,0:T(8,128)S(1)} %get-tuple-element.16.doc_ref, f32[128,4]{1,0:T(8,128)S(1)} %bitcast.11), custom_call_target="tpu_custom_call" | custom-call | tf_op jit(solution)/shard_map/unpack/pallas_call | solution.py:336
Async XLA Ops:
  29.7 11.0 %collective-permute-start.4 = (bf16[64,4,1024]{2,1,0:T(4,128)(2,1)S(1)}, bf16[64,4,1024]{2,1,0:T(4,128)(2,1)S(1)}, u32[]{:S(2)}, u32[]{:S(2)}) collective-permute-start(bf16[64,4,1024]{2,1,0:T(4,128)(2,1)S(1)} %all_to_all.16.direct_ref), channel_id=1, source_target_pairs={{0,1},{2,3},{4,5},{6,7},{8,9},{10,11},{12,13},{14,15},{16,17},{18,... | collective-permute-start | bytes 1572872 | tf_op jit(solution)/shard_map/ppermute | solution.py:319
  31.9 5.8 %collective-permute-start = (bf16[32,4,1024]{2,1,0:T(4,128)(2,1)S(1)}, bf16[32,4,1024]{2,1,0:T(4,128)(2,1)S(1)}, u32[]{:S(2)}, u32[]{:S(2)}) collective-permute-start(bf16[32,4,1024]{2,1,0:T(4,128)(2,1)S(1)} %get-tuple-element.28), channel_id=1, source_target_pairs={{8,0},{10,2},{12,4},{14,6},{0,8},{2,10},{4,12},{6,14},{24,16},{26,... | collective-permute-start | bytes 786440 | tf_op jit(solution)/shard_map/ppermute | solution.py:316
  33.7 6.4 %collective-permute-start.1 = (bf16[32,4,1024]{2,1,0:T(4,128)(2,1)S(1)}, bf16[32,4,1024]{2,1,0:T(4,128)(2,1)S(1)}, u32[]{:S(2)}, u32[]{:S(2)}) collective-permute-start(bf16[32,4,1024]{2,1,0:T(4,128)(2,1)S(1)} %get-tuple-element.27), channel_id=1, source_target_pairs={{32,0},{34,2},{36,4},{38,6},{40,8},{42,10},{44,12},{46,14},{48,16}... | collective-permute-start | bytes 786440 | tf_op jit(solution)/shard_map/ppermute | solution.py:315
  40.1 1.8 %collective-permute-start.3 = (bf16[32,4,1024]{2,1,0:T(4,128)(2,1)S(1)}, bf16[32,4,1024]{2,1,0:T(4,128)(2,1)S(1)}, u32[]{:S(2)}, u32[]{:S(2)}) collective-permute-start(bf16[32,4,1024]{2,1,0:T(4,128)(2,1)S(1)} %collective-permute-done.1.high_ref), channel_id=1, source_target_pairs={{0,1},{2,3},{4,5},{6,7},{8,9},{10,11},{12,13},{14,15},{16,17},{18,... | collective-permute-start | bytes 786440 | tf_op jit(solution)/shard_map/ppermute | solution.py:324
  40.7 1.5 %collective-permute-start.2 = (bf16[32,4,1024]{2,1,0:T(4,128)(2,1)S(1)}, bf16[32,4,1024]{2,1,0:T(4,128)(2,1)S(1)}, u32[]{:S(2)}, u32[]{:S(2)}) collective-permute-start(bf16[32,4,1024]{2,1,0:T(4,128)(2,1)S(1)} %collective-permute-done.low_ref), channel_id=1, source_target_pairs={{0,1},{2,3},{4,5},{6,7},{8,9},{10,11},{12,13},{14,15},{16,17},{18,... | collective-permute-start | bytes 786440 | tf_op jit(solution)/shard_map/ppermute | solution.py:322

commit v8 on v7

--- a/solution.py
+++ b/solution.py
@@ -117,19 +117,19 @@
     row, spot = iota((rows, 4 * clusters), 0), iota((rows, 4 * clusters), 1)
     spread = (spot == (row & 3) * clusters + 2 * (listed(row >> 2) ^ flip)).astype(BF16)
     last = (((1,), (1,)), ((), ()))
+    copies[2].wait()
     pick = lax.dot_general(
         spread, jnp.concatenate(hits, axis=1), last, preferred_element_type=F32
     ).astype(BF16)
-    take_pair = iota((pairs, clusters), 1) == 2 * listed(iota((pairs, clusters), 0))
-    doc_ref[...] = lax.dot_general(
-        take_pair.astype(BF16), picked.astype(BF16), last, preferred_element_type=F32
-    ).astype(I32)
-    copies[2].wait()
     emb = emb_ref[...]
     square = jnp.sum(emb * emb, axis=1, keepdims=True)
     normed = (emb * lax.rsqrt(square + 1e-06)).astype(BF16)
     packed = jnp.dot(pick, normed, preferred_element_type=F32).astype(BF16)
     packed_ref[...] = packed.reshape(packed_ref.shape)
+    take_pair = iota((pairs, clusters), 1) == 2 * listed(iota((pairs, clusters), 0))
+    doc_ref[...] = lax.dot_general(
+        take_pair.astype(BF16), picked.astype(BF16), last, preferred_element_type=F32
+    ).astype(I32)
 
 
 def in_hbm(array):
@@ -234,29 +234,56 @@
     best_ref[...] = jnp.broadcast_to(best, best_ref.shape)
 
 
-def passed_kernel(
-    row_ref, col_ref, direct_ref, direct_other_ref, low_ref, high_ref, best_direct_ref, best_ref
+def low_kernel(row_ref, col_ref, direct_ref, direct_other_ref, low_ref, before_ref, best_ref):
+    end = 256 + 4 * LOW
+    direct, low = rows_of(direct_ref), rows_of(low_ref)
+    own = jnp.concatenate([direct, low], axis=0)
+    label = row_ref[0:1, 0:end]
+    best = jnp.maximum(
+        column_best(low, own, col_ref[256:end, 0:1], label, 256),
+        column_best(rows_of(direct_other_ref), own, col_ref[512:768, 0:1], label),
+    )
+    best_low = column_best(direct, low, col_ref[0:256, 0:1], row_ref[0:1, 256:end])
+    best = jnp.maximum(best, jnp.concatenate([before_ref[0:1, :], best_low], axis=1))
+    best_ref[...] = jnp.broadcast_to(best, best_ref.shape)
+
+
+def high_kernel(
+    row_ref,
+    col_ref,
+    direct_ref,
+    direct_other_ref,
+    low_ref,
+    low_other_ref,
+    high_ref,
+    before_ref,
+    best_ref,
 ):
-    direct, passed = rows_of(direct_ref), rows_of(low_ref, high_ref)
-    own = jnp.concatenate([direct, passed], axis=0)
+    start = 256 + 4 * LOW
+    earlier, high = rows_of(direct_ref, low_ref), rows_of(high_ref)
+    own = jnp.concatenate([earlier, high], axis=0)
     best = jnp.maximum(
-        column_best(passed, own, col_ref[256:512, 0:1], row_ref[0:1, :], 256),
-        column_best(rows_of(direct_other_ref), own, col_ref[512:768, 0:1], row_ref[0:1, :]),
-    )
-    best_passed = column_best(direct, passed, col_ref[0:256, 0:1], row_ref[0:1, 256:512])
-    best = jnp.maximum(
-        best, jnp.concatenate([best_direct_ref[0:1, :], best_passed], axis=1)
-    )
+        column_best(high, own, col_ref[start:512, 0:1], row_ref[0:1, :], start),
+        column_best(rows_of(low_other_ref), own, col_ref[768 : start + 512, 0:1], row_ref[0:1, :]),
+    )
+    label = row_ref[0:1, start:512]
+    best_high = jnp.maximum(
+        column_best(earlier, high, col_ref[0:start, 0:1], label),
+        column_best(rows_of(direct_other_ref), high, col_ref[512:768, 0:1], label),
+    )
+    best = jnp.maximum(best, jnp.concatenate([before_ref[0:1, :], best_high], axis=1))
     best_ref[...] = jnp.broadcast_to(best, best_ref.shape)
 
 
 def final_kernel(
-    row_ref, col_ref, direct_ref, low_ref, high_ref, low_other_ref, high_other_ref, best_ref, back_ref
+    row_ref, col_ref, direct_ref, low_ref, high_ref, high_other_ref, before_ref, back_ref
 ):
+    start = 256 + 4 * LOW
     own = rows_of(direct_ref, low_ref, high_ref)
-    others = rows_of(low_other_ref, high_other_ref)
-    best = column_best(others, own, col_ref[768:1024, 0:1], row_ref[0:1, :])
-    best = jnp.maximum(best, best_ref[0:1, :])
+    best = column_best(
+        rows_of(high_other_ref), own, col_ref[start + 512 : 1024, 0:1], row_ref[0:1, :]
+    )
+    best = jnp.maximum(best, before_ref[0:1, :])
     slot, member = iota((128, 512), 0), iota((128, 512), 1)
     spread = jnp.where(member // 4 == slot, jnp.broadcast_to(best, (128, 512)), -1.0)
     for rank in range(4):
@@ -318,17 +345,20 @@
     row, col = labels(late_ids, late_counts)
     direct_other = lax.ppermute(direct, BOTH, swap)
     best = vmem_call(direct_kernel, (8, 256), "score_direct", 10**9, row, col, direct)
-    low, best = lax.optimization_barrier((low, best))
     low_other = lax.ppermute(low, BOTH, swap)
+    best = vmem_call(
+        low_kernel, (8, 256 + 4 * LOW), "score_low", 10**9,
+        row, col, direct, direct_other, low, best,
+    )
     high, best = lax.optimization_barrier((high, best))
     high_other = lax.ppermute(high, BOTH, swap)
     best = vmem_call(
-        passed_kernel, (8, 512), "score_passed", 10**9,
-        row, col, direct, direct_other, low, high, best,
+        high_kernel, (8, 512), "score_high", 10**9,
+        row, col, direct, direct_other, low, low_other, high, best,
     )
     best = vmem_call(
         final_kernel, (128, 4), "score_final", 10**9,
-        row, col, direct, low, high, low_other, high_other, best,
+        row, col, direct, low, high, high_other, best,
     )
     back = lax.all_to_all(
         best, BOTH, split_axis=0, concat_axis=0, axis_index_groups=back_groups, tiled=True

time: 59.1 us -> 59 us (level)
  waiting for transfers between devices: 3.76 us -> 1.33 us
  Pallas kernels: 6.23 us -> 7.22 us
  starting transfers between devices: 6.04 us -> 6.99 us
    ppermute x1, waiting for transfers between devices: 2.38 us -> 0.56 us  [body(): high = lax.ppermute(direct[LOW:], BOTH, high_route)]
    pallas_call x3 -> x4, Pallas kernels: 1.89 us -> 3.02 us  [vmem_call(): pl.pallas_call(kernel, out_shape=jax.ShapeDtypeStruct(shape, F32), in_spe...]
    ppermute x1, starting transfers between devices: 0.01 us -> 0.96 us  [body(): low_other = lax.ppermute(low, BOTH, swap)]
  transfers between devices with their start and end apart: 5 -> 5, of which waited for: 4 -> 2; matrix products, arithmetic and copies ran while one was open for 0% -> 0% of each run, Pallas kernels for 4% -> 6%
where the time goes in v8:
time: 59 us; the launch traced here: 58.7 us
  blocking collectives  42.9 us (73%)
  Pallas kernels  7.22 us (12%)
  starting transfers between devices  6.99 us (12%)
  waiting for transfers between devices  1.33 us (2%)
    all_to_all x1, blocking collectives, body(): lax.all_to_all(packed, BOTH, split_axis=0, concat_axis=0, axis_index_grou...  27.3 us
    all_to_all x1, blocking collectives, body(): lax.all_to_all(best, BOTH, split_axis=0, concat_axis=0, axis_index_groups...  15.6 us
    pallas_call x4, Pallas kernels, vmem_call(): pl.pallas_call(kernel, out_shape=jax.ShapeDtypeStruct(shape, F32), in_spe...  3.02 us
    pallas_call x1, Pallas kernels, pack(): pl.pallas_call(pack_kernel, out_shape=(jax.ShapeDtypeStruct((clusters //...  2.22 us
    ppermute x1, starting transfers between devices, body(): direct_other = lax.ppermute(direct, BOTH, swap)  2.05 us
    ppermute x1, starting transfers between devices, body(): low = lax.ppermute(direct[:LOW], BOTH, low_route)  1.72 us
    ppermute x1, starting transfers between devices, body(): high = lax.ppermute(direct[LOW:], BOTH, high_route)  1.66 us
    pallas_call x1, Pallas kernels, labels(): pl.pallas_call(label_kernel, out_shape=(jax.ShapeDtypeStruct((8, 512), F3...  1.27 us
  transfers between devices with their start and end apart: 5, of which 2 were waited for; matrix products, arithmetic and copies ran while one was open for 0% of the time, Pallas kernels for 6%

profile of v8, /device:TPU:1, one launch (start us, length us, event | category | flops | bytes accessed | tf_op | source)
XLA Modules:
  0.0 58.7 jit_solution(7806880762546468897)
XLA Ops:
  0.0 2.2 %pack.1 = (bf16[64,4,1024]{2,1,0:T(4,128)(2,1)S(1)}, s32[64,128]{1,0:T(8,128)S(1)}) custom-call(f32[256,1024]{1,0:T(8,128)} %emb_hbm.1, s32[1024,128]{1,0:T(8,128)} %bitcast.13, s32[1,128]{1,0:T(1,128)} %bitcast.14), custom_call_target="tpu_custom_call" | custom-call | tf_op jit(solution)/shard_map/pack/pallas_call | solution.py:146
  2.2 27.3 %all_to_all.16.direct_ref = bf16[64,4,1024]{2,1,0:T(4,128)(2,1)S(1)} all-to-all(bf16[64,4,1024]{2,1,0:T(4,128)(2,1)S(1)} %get-tuple-element.15), channel_id=1, replica_groups={{148,154,158,162,166,168,172,178,182,184,188,192,196,202,206,208,212,21..., dimensions={0} | all-to-all | bytes 1048576 | tf_op jit(solution)/shard_map/all_to_all | solution.py:339
  29.6 2.1 %collective-permute-start.2 = (bf16[64,4,1024]{2,1,0:T(4,128)(2,1)S(1)}, bf16[64,4,1024]{2,1,0:T(4,128)(2,1)S(1)}, u32[]{:S(2)}, u32[]{:S(2)}) collective-permute-start(bf16[64,4,1024]{2,1,0:T(4,128)(2,1)S(1)} %all_to_all.16.direct_ref), channel_id=1, source_target_pairs={{0,1},{2,3},{4,5},{6,7},{8,9},{10,11},{12,13},{14,15},{16,17},{18,... | collective-permute-start | bytes 1572872 | tf_op jit(solution)/shard_map/ppermute | solution.py:346
  31.6 0.2 fusion
  31.8 1.7 %collective-permute-start = (bf16[32,4,1024]{2,1,0:T(4,128)(2,1)S(1)}, bf16[32,4,1024]{2,1,0:T(4,128)(2,1)S(1)}, u32[]{:S(2)}, u32[]{:S(2)}) collective-permute-start(bf16[32,4,1024]{2,1,0:T(4,128)(2,1)S(1)} %get-tuple-element.24), channel_id=1, source_target_pairs={{8,0},{10,2},{12,4},{14,6},{0,8},{2,10},{4,12},{6,14},{24,16},{26,... | collective-permute-start | bytes 786440 | tf_op jit(solution)/shard_map/ppermute | solution.py:343
  33.5 1.7 %collective-permute-start.1 = (bf16[32,4,1024]{2,1,0:T(4,128)(2,1)S(1)}, bf16[32,4,1024]{2,1,0:T(4,128)(2,1)S(1)}, u32[]{:S(2)}, u32[]{:S(2)}) collective-permute-start(bf16[32,4,1024]{2,1,0:T(4,128)(2,1)S(1)} %get-tuple-element.23), channel_id=1, source_target_pairs={{32,0},{34,2},{36,4},{38,6},{40,8},{42,10},{44,12},{46,14},{48,16}... | collective-permute-start | bytes 786440 | tf_op jit(solution)/shard_map/ppermute | solution.py:342
  35.2 1.3 %labels.1 = (f32[8,512]{1,0:T(8,128)S(1)}, f32[1024,128]{1,0:T(8,128)S(1)}) custom-call(s32[128,2,512]{2,1,0:T(2,128)} %ids_hbm, s32[1,128]{1,0:T(1,128)} %bitcast.15), custom_call_target="tpu_custom_call" | custom-call | flops 1000000000 | bytes 4194304 | tf_op jit(solution)/shard_map/labels/pallas_call | solution.py:199
  36.5 0.3 score_direct.1.before_ref
  36.8 0.8 %collective-permute-done.low_ref = bf16[32,4,1024]{2,1,0:T(4,128)(2,1)S(1)} collective-permute-done((bf16[32,4,1024]{2,1,0:T(4,128)(2,1)S(1)}, bf16[32,4,1024]{2,1,0:T(4,128)(2,1)S(1)}, u32[]{:S(2)}, u32[]{:S(2)}) %collective-permute-start) | collective-permute-done | bytes 262176 | tf_op jit(solution)/shard_map/ppermute | solution.py:343
  37.6 1.0 %collective-permute-start.4 = (bf16[32,4,1024]{2,1,0:T(4,128)(2,1)S(1)}, bf16[32,4,1024]{2,1,0:T(4,128)(2,1)S(1)}, u32[]{:S(2)}, u32[]{:S(2)}) collective-permute-start(bf16[32,4,1024]{2,1,0:T(4,128)(2,1)S(1)} %collective-permute-done.low_ref), channel_id=1, source_target_pairs={{0,1},{2,3},{4,5},{6,7},{8,9},{10,11},{12,13},{14,15},{16,17},{18,... | collective-permute-start | bytes 786440 | tf_op jit(solution)/shard_map/ppermute | solution.py:348
  38.5 0.0 collective-permute-done.2.direct_other_ref
  38.5 0.9 %score_low.1.before_ref = f32[8,384]{1,0:T(8,128)S(1)} custom-call(f32[8,512]{1,0:T(8,128)S(1)} %get-tuple-element.18.row_ref, f32[1024,128]{1,0:T(8,128)S(1)} %get-tuple-element.19.col_ref, bf16[64,4,1024]{2,1,0:T(4,128)(2,1)S(1)} %all_to_all.16.direct_ref, bf16[64,4,1024]{2,1,0:T(4,128)(2,1)S(1)} %collective-permute-done.2.direct_other_ref, ...), custom_call_target="tpu_custom_call" | custom-call | flops 1000000000 | bytes 2097152 | tf_op jit(solution)/shard_map/score_low/pallas_call | solution.py:296
  39.4 0.6 collective-permute-done.1.high_ref
  39.9 0.6 %collective-permute-start.3 = (bf16[32,4,1024]{2,1,0:T(4,128)(2,1)S(1)}, bf16[32,4,1024]{2,1,0:T(4,128)(2,1)S(1)}, u32[]{:S(2)}, u32[]{:S(2)}) collective-permute-start(bf16[32,4,1024]{2,1,0:T(4,128)(2,1)S(1)} %collective-permute-done.1.high_ref), channel_id=1, source_target_pairs={{0,1},{2,3},{4,5},{6,7},{8,9},{10,11},{12,13},{14,15},{16,17},{18,... | collective-permute-start | bytes 786440 | tf_op jit(solution)/shard_map/ppermute | solution.py:354
  40.6 0.0 collective-permute-done.4.low_other_ref
  40.6 1.2 %score_high.1.before_ref = f32[8,512]{1,0:T(8,128)S(1)} custom-call(f32[8,512]{1,0:T(8,128)S(1)} %get-tuple-element.18.row_ref, f32[1024,128]{1,0:T(8,128)S(1)} %get-tuple-element.19.col_ref, bf16[64,4,1024]{2,1,0:T(4,128)(2,1)S(1)} %all_to_all.16.direct_ref, bf16[64,4,1024]{2,1,0:T(4,128)(2,1)S(1)} %collective-permute-done.2.direct_other_ref, ...), custom_call_target="tpu_custom_call" | custom-call | flops 1000000000 | bytes 2097152 | tf_op jit(solution)/shard_map/score_high/pallas_call | solution.py:296
  41.7 0.0 collective-permute-done.3.high_other_ref
  41.7 0.6 %score_final.1 = f32[128,4]{1,0:T(8,128)S(1)} custom-call(f32[8,512]{1,0:T(8,128)S(1)} %get-tuple-element.18.row_ref, f32[1024,128]{1,0:T(8,128)S(1)} %get-tuple-element.19.col_ref, bf16[64,4,1024]{2,1,0:T(4,128)(2,1)S(1)} %all_to_all.16.direct_ref, bf16[32,4,1024]{2,1,0:T(4,128)(2,1)S(1)} %collective-permute-done.low_ref, ...), custom_call_target="tpu_custom_call" | custom-call | flops 1000000000 | bytes 2097152 | tf_op jit(solution)/shard_map/score_final/pallas_call | solution.py:296
  42.4 15.6 %all_to_all.17 = f32[128,1,4]{2,1,0:T(1,128)S(1)} all-to-all(f32[128,1,4]{2,1,0:T(1,128)S(1)} %bitcast.12), channel_id=1, replica_groups={{148,154,158,162,166,168,172,178,182,184,188,192,196,202,206,208,212,21..., dimensions={0} | all-to-all | bytes 4096 | tf_op jit(solution)/shard_map/all_to_all | solution.py:363
  58.0 0.7 %unpack.1 = f32[1,256]{1,0:T(1,128)} custom-call(s32[64,128]{1,0:T(8,128)S(1)} %get-tuple-element.14.doc_ref, f32[128,4]{1,0:T(8,128)S(1)} %bitcast.11), custom_call_target="tpu_custom_call" | custom-call | tf_op jit(solution)/shard_map/unpack/pallas_call | solution.py:366
Async XLA Ops:
  29.6 9.0 %collective-permute-start.2 = (bf16[64,4,1024]{2,1,0:T(4,128)(2,1)S(1)}, bf16[64,4,1024]{2,1,0:T(4,128)(2,1)S(1)}, u32[]{:S(2)}, u32[]{:S(2)}) collective-permute-start(bf16[64,4,1024]{2,1,0:T(4,128)(2,1)S(1)} %all_to_all.16.direct_ref), channel_id=1, source_target_pairs={{0,1},{2,3},{4,5},{6,7},{8,9},{10,11},{12,13},{14,15},{16,17},{18,... | collective-permute-start | bytes 1572872 | tf_op jit(solution)/shard_map/ppermute | solution.py:346
  31.8 5.8 %collective-permute-start = (bf16[32,4,1024]{2,1,0:T(4,128)(2,1)S(1)}, bf16[32,4,1024]{2,1,0:T(4,128)(2,1)S(1)}, u32[]{:S(2)}, u32[]{:S(2)}) collective-permute-start(bf16[32,4,1024]{2,1,0:T(4,128)(2,1)S(1)} %get-tuple-element.24), channel_id=1, source_target_pairs={{8,0},{10,2},{12,4},{14,6},{0,8},{2,10},{4,12},{6,14},{24,16},{26,... | collective-permute-start | bytes 786440 | tf_op jit(solution)/shard_map/ppermute | solution.py:343
  33.5 6.4 %collective-permute-start.1 = (bf16[32,4,1024]{2,1,0:T(4,128)(2,1)S(1)}, bf16[32,4,1024]{2,1,0:T(4,128)(2,1)S(1)}, u32[]{:S(2)}, u32[]{:S(2)}) collective-permute-start(bf16[32,4,1024]{2,1,0:T(4,128)(2,1)S(1)} %get-tuple-element.23), channel_id=1, source_target_pairs={{32,0},{34,2},{36,4},{38,6},{40,8},{42,10},{44,12},{46,14},{48,16}... | collective-permute-start | bytes 786440 | tf_op jit(solution)/shard_map/ppermute | solution.py:342
  37.6 3.0 %collective-permute-start.4 = (bf16[32,4,1024]{2,1,0:T(4,128)(2,1)S(1)}, bf16[32,4,1024]{2,1,0:T(4,128)(2,1)S(1)}, u32[]{:S(2)}, u32[]{:S(2)}) collective-permute-start(bf16[32,4,1024]{2,1,0:T(4,128)(2,1)S(1)} %collective-permute-done.low_ref), channel_id=1, source_target_pairs={{0,1},{2,3},{4,5},{6,7},{8,9},{10,11},{12,13},{14,15},{16,17},{18,... | collective-permute-start | bytes 786440 | tf_op jit(solution)/shard_map/ppermute | solution.py:348
  39.9 1.8 %collective-permute-start.3 = (bf16[32,4,1024]{2,1,0:T(4,128)(2,1)S(1)}, bf16[32,4,1024]{2,1,0:T(4,128)(2,1)S(1)}, u32[]{:S(2)}, u32[]{:S(2)}) collective-permute-start(bf16[32,4,1024]{2,1,0:T(4,128)(2,1)S(1)} %collective-permute-done.1.high_ref), channel_id=1, source_target_pairs={{0,1},{2,3},{4,5},{6,7},{8,9},{10,11},{12,13},{14,15},{16,17},{18,... | collective-permute-start | bytes 786440 | tf_op jit(solution)/shard_map/ppermute | solution.py:354

commit v9 on v8

--- a/solution.py
+++ b/solution.py
@@ -258,10 +258,12 @@
     high_ref,
     before_ref,
     best_ref,
+    own_ref,
 ):
     start = 256 + 4 * LOW
     earlier, high = rows_of(direct_ref, low_ref), rows_of(high_ref)
     own = jnp.concatenate([earlier, high], axis=0)
+    own_ref[...] = jnp.transpose(own)
     best = jnp.maximum(
         column_best(high, own, col_ref[start:512, 0:1], row_ref[0:1, :], start),
         column_best(rows_of(low_other_ref), own, col_ref[768 : start + 512, 0:1], row_ref[0:1, :]),
@@ -275,14 +277,11 @@
     best_ref[...] = jnp.broadcast_to(best, best_ref.shape)
 
 
-def final_kernel(
-    row_ref, col_ref, direct_ref, low_ref, high_ref, high_other_ref, before_ref, back_ref
-):
+def final_kernel(row_ref, col_ref, own_ref, high_other_ref, before_ref, back_ref):
     start = 256 + 4 * LOW
-    own = rows_of(direct_ref, low_ref, high_ref)
-    best = column_best(
-        rows_of(high_other_ref), own, col_ref[start + 512 : 1024, 0:1], row_ref[0:1, :]
-    )
+    scores = jnp.dot(rows_of(high_other_ref), own_ref[...], preferred_element_type=F32)
+    same = col_ref[start + 512 : 1024, 0:1] == row_ref[0:1, :]
+    best = jnp.max(jnp.where(same, scores, -1.0), axis=0, keepdims=True)
     best = jnp.maximum(best, before_ref[0:1, :])
     slot, member = iota((128, 512), 0), iota((128, 512), 1)
     spread = jnp.where(member // 4 == slot, jnp.broadcast_to(best, (128, 512)), -1.0)
@@ -292,12 +291,16 @@
         )
 
 
-def vmem_call(kernel, shape, name, flops, *operands):
+def vmem_call(kernel, shape, name, flops, *operands, wide=None):
+    shapes = jax.ShapeDtypeStruct(shape, F32)
+    places = in_vmem(1)[0]
+    if wide is not None:
+        shapes, places = (shapes, jax.ShapeDtypeStruct(wide, BF16)), tuple(in_vmem(2))
     return pl.pallas_call(
         kernel,
-        out_shape=jax.ShapeDtypeStruct(shape, F32),
+        out_shape=shapes,
         in_specs=in_vmem(len(operands)),
-        out_specs=in_vmem(1)[0],
+        out_specs=places,
         compiler_params=pltpu.CompilerParams(vmem_limit_bytes=16 * MIB),
         cost_estimate=pl.CostEstimate(flops=flops, bytes_accessed=2 * MIB, transcendentals=0),
         name=name,
@@ -352,13 +355,14 @@
     )
     high, best = lax.optimization_barrier((high, best))
     high_other = lax.ppermute(high, BOTH, swap)
-    best = vmem_call(
+    best, own = vmem_call(
         high_kernel, (8, 512), "score_high", 10**9,
         row, col, direct, direct_other, low, low_other, high, best,
+        wide=(direct.shape[2], 512),
     )
     best = vmem_call(
         final_kernel, (128, 4), "score_final", 10**9,
-        row, col, direct, low, high, high_other, best,
+        row, col, own, high_other, best,
     )
     back = lax.all_to_all(
         best, BOTH, split_axis=0, concat_axis=0, axis_index_groups=back_groups, tiled=True

time: 59 us -> 58.9 us (level)
  no operation moved by 1% of the time
where the time goes in v9:
time: 58.9 us; the launch traced here: 58.5 us
  blocking collectives  42.9 us (73%)
  Pallas kernels  7.06 us (12%)
  starting transfers between devices  6.99 us (12%)
  waiting for transfers between devices  1.33 us (2%)
    all_to_all x1, blocking collectives, body(): lax.all_to_all(packed, BOTH, split_axis=0, concat_axis=0, axis_index_grou...  27.3 us
    all_to_all x1, blocking collectives, body(): lax.all_to_all(best, BOTH, split_axis=0, concat_axis=0, axis_index_groups...  15.6 us
    pallas_call x4, Pallas kernels, vmem_call(): pl.pallas_call(kernel, out_shape=shapes, in_specs=in_vmem(len(operands)),...  2.86 us
    pallas_call x1, Pallas kernels, pack(): pl.pallas_call(pack_kernel, out_shape=(jax.ShapeDtypeStruct((clusters //...  2.22 us
    ppermute x1, starting transfers between devices, body(): direct_other = lax.ppermute(direct, BOTH, swap)  2.05 us
    ppermute x1, starting transfers between devices, body(): low = lax.ppermute(direct[:LOW], BOTH, low_route)  1.72 us
    ppermute x1, starting transfers between devices, body(): high = lax.ppermute(direct[LOW:], BOTH, high_route)  1.66 us
    pallas_call x1, Pallas kernels, labels(): pl.pallas_call(label_kernel, out_shape=(jax.ShapeDtypeStruct((8, 512), F3...  1.27 us
  transfers between devices with their start and end apart: 5, of which 2 were waited for; matrix products, arithmetic and copies ran while one was open for 0% of the time, Pallas kernels for 6%

profile of v9, /device:TPU:1, one launch (start us, length us, event | category | flops | bytes accessed | tf_op | source)
XLA Modules:
  0.0 58.5 jit_solution(4824447780510656751)
XLA Ops:
  0.0 2.2 %pack.1 = (bf16[64,4,1024]{2,1,0:T(4,128)(2,1)S(1)}, s32[64,128]{1,0:T(8,128)S(1)}) custom-call(f32[256,1024]{1,0:T(8,128)} %emb_hbm.1, s32[1024,128]{1,0:T(8,128)} %bitcast.13, s32[1,128]{1,0:T(1,128)} %bitcast.14), custom_call_target="tpu_custom_call" | custom-call | tf_op jit(solution)/shard_map/pack/pallas_call | solution.py:146
  2.2 27.3 %all_to_all.16.direct_ref = bf16[64,4,1024]{2,1,0:T(4,128)(2,1)S(1)} all-to-all(bf16[64,4,1024]{2,1,0:T(4,128)(2,1)S(1)} %get-tuple-element.17), channel_id=1, replica_groups={{148,154,158,162,166,168,172,178,182,184,188,192,196,202,206,208,212,21..., dimensions={0} | all-to-all | bytes 1048576 | tf_op jit(solution)/shard_map/all_to_all | solution.py:342
  29.6 2.1 %collective-permute-start = (bf16[64,4,1024]{2,1,0:T(4,128)(2,1)S(1)}, bf16[64,4,1024]{2,1,0:T(4,128)(2,1)S(1)}, u32[]{:S(2)}, u32[]{:S(2)}) collective-permute-start(bf16[64,4,1024]{2,1,0:T(4,128)(2,1)S(1)} %all_to_all.16.direct_ref), channel_id=1, source_target_pairs={{0,1},{2,3},{4,5},{6,7},{8,9},{10,11},{12,13},{14,15},{16,17},{18,... | collective-permute-start | bytes 1572872 | tf_op jit(solution)/shard_map/ppermute | solution.py:349
  31.6 0.2 fusion
  31.8 1.7 %collective-permute-start.1 = (bf16[32,4,1024]{2,1,0:T(4,128)(2,1)S(1)}, bf16[32,4,1024]{2,1,0:T(4,128)(2,1)S(1)}, u32[]{:S(2)}, u32[]{:S(2)}) collective-permute-start(bf16[32,4,1024]{2,1,0:T(4,128)(2,1)S(1)} %get-tuple-element.28), channel_id=1, source_target_pairs={{8,0},{10,2},{12,4},{14,6},{0,8},{2,10},{4,12},{6,14},{24,16},{26,... | collective-permute-start | bytes 786440 | tf_op jit(solution)/shard_map/ppermute | solution.py:346
  33.5 1.7 %collective-permute-start.3 = (bf16[32,4,1024]{2,1,0:T(4,128)(2,1)S(1)}, bf16[32,4,1024]{2,1,0:T(4,128)(2,1)S(1)}, u32[]{:S(2)}, u32[]{:S(2)}) collective-permute-start(bf16[32,4,1024]{2,1,0:T(4,128)(2,1)S(1)} %get-tuple-element.27), channel_id=1, source_target_pairs={{32,0},{34,2},{36,4},{38,6},{40,8},{42,10},{44,12},{46,14},{48,16}... | collective-permute-start | bytes 786440 | tf_op jit(solution)/shard_map/ppermute | solution.py:345
  35.2 1.3 %labels.1 = (f32[8,512]{1,0:T(8,128)S(1)}, f32[1024,128]{1,0:T(8,128)S(1)}) custom-call(s32[128,2,512]{2,1,0:T(2,128)} %ids_hbm, s32[1,128]{1,0:T(1,128)} %bitcast.15), custom_call_target="tpu_custom_call" | custom-call | flops 1000000000 | bytes 4194304 | tf_op jit(solution)/shard_map/labels/pallas_call | solution.py:199
  36.5 0.3 score_direct.1.before_ref
  36.8 0.8 %collective-permute-done.1.low_ref = bf16[32,4,1024]{2,1,0:T(4,128)(2,1)S(1)} collective-permute-done((bf16[32,4,1024]{2,1,0:T(4,128)(2,1)S(1)}, bf16[32,4,1024]{2,1,0:T(4,128)(2,1)S(1)}, u32[]{:S(2)}, u32[]{:S(2)}) %collective-permute-start.1) | collective-permute-done | bytes 262176 | tf_op jit(solution)/shard_map/ppermute | solution.py:346
  37.6 1.0 %collective-permute-start.2 = (bf16[32,4,1024]{2,1,0:T(4,128)(2,1)S(1)}, bf16[32,4,1024]{2,1,0:T(4,128)(2,1)S(1)}, u32[]{:S(2)}, u32[]{:S(2)}) collective-permute-start(bf16[32,4,1024]{2,1,0:T(4,128)(2,1)S(1)} %collective-permute-done.1.low_ref), channel_id=1, source_target_pairs={{0,1},{2,3},{4,5},{6,7},{8,9},{10,11},{12,13},{14,15},{16,17},{18,... | collective-permute-start | bytes 786440 | tf_op jit(solution)/shard_map/ppermute | solution.py:351
  38.5 0.0 collective-permute-done.direct_other_ref
  38.5 0.9 %score_low.1.before_ref = f32[8,384]{1,0:T(8,128)S(1)} custom-call(f32[8,512]{1,0:T(8,128)S(1)} %get-tuple-element.20.row_ref, f32[1024,128]{1,0:T(8,128)S(1)} %get-tuple-element.21.col_ref, bf16[64,4,1024]{2,1,0:T(4,128)(2,1)S(1)} %all_to_all.16.direct_ref, bf16[64,4,1024]{2,1,0:T(4,128)(2,1)S(1)} %collective-permute-done.direct_other_ref, ...), custom_call_target="tpu_custom_call" | custom-call | flops 1000000000 | bytes 2097152 | tf_op jit(solution)/shard_map/score_low/pallas_call | solution.py:299
  39.4 0.6 collective-permute-done.3.high_ref
  39.9 0.6 %collective-permute-start.4 = (bf16[32,4,1024]{2,1,0:T(4,128)(2,1)S(1)}, bf16[32,4,1024]{2,1,0:T(4,128)(2,1)S(1)}, u32[]{:S(2)}, u32[]{:S(2)}) collective-permute-start(bf16[32,4,1024]{2,1,0:T(4,128)(2,1)S(1)} %collective-permute-done.3.high_ref), channel_id=1, source_target_pairs={{0,1},{2,3},{4,5},{6,7},{8,9},{10,11},{12,13},{14,15},{16,17},{18,... | collective-permute-start | bytes 786440 | tf_op jit(solution)/shard_map/ppermute | solution.py:357
  40.6 0.0 collective-permute-done.2.low_other_ref
  40.6 1.2 %score_high.1 = (f32[8,512]{1,0:T(8,128)S(1)}, bf16[1024,512]{1,0:T(8,128)(2,1)S(1)}) custom-call(f32[8,512]{1,0:T(8,128)S(1)} %get-tuple-element.20.row_ref, f32[1024,128]{1,0:T(8,128)S(1)} %get-tuple-element.21.col_ref, bf16[64,4,1024]{2,1,0:T(4,128)(2,1)S(1)} %all_to_all.16.direct_ref, bf16[64,4,1024]{2,1,0:T(4,128)(2,1)S(1)} %collective-permute-done.direct_other_ref, ...), custom_call_target="tpu_custom_call" | custom-call | flops 1000000000 | bytes 2097152 | tf_op jit(solution)/shard_map/score_high/pallas_call | solution.py:299
  41.8 0.0 collective-permute-done.4.high_other_ref
  41.8 0.5 score_final.1
  42.2 15.6 %all_to_all.17 = f32[128,1,4]{2,1,0:T(1,128)S(1)} all-to-all(f32[128,1,4]{2,1,0:T(1,128)S(1)} %bitcast.12), channel_id=1, replica_groups={{148,154,158,162,166,168,172,178,182,184,188,192,196,202,206,208,212,21..., dimensions={0} | all-to-all | bytes 4096 | tf_op jit(solution)/shard_map/all_to_all | solution.py:367
  57.8 0.7 %unpack.1 = f32[1,256]{1,0:T(1,128)} custom-call(s32[64,128]{1,0:T(8,128)S(1)} %get-tuple-element.16.doc_ref, f32[128,4]{1,0:T(8,128)S(1)} %bitcast.11), custom_call_target="tpu_custom_call" | custom-call | tf_op jit(solution)/shard_map/unpack/pallas_call | solution.py:370
Async XLA Ops:
  29.6 9.0 %collective-permute-start = (bf16[64,4,1024]{2,1,0:T(4,128)(2,1)S(1)}, bf16[64,4,1024]{2,1,0:T(4,128)(2,1)S(1)}, u32[]{:S(2)}, u32[]{:S(2)}) collective-permute-start(bf16[64,4,1024]{2,1,0:T(4,128)(2,1)S(1)} %all_to_all.16.direct_ref), channel_id=1, source_target_pairs={{0,1},{2,3},{4,5},{6,7},{8,9},{10,11},{12,13},{14,15},{16,17},{18,... | collective-permute-start | bytes 1572872 | tf_op jit(solution)/shard_map/ppermute | solution.py:349
  31.8 5.8 %collective-permute-start.1 = (bf16[32,4,1024]{2,1,0:T(4,128)(2,1)S(1)}, bf16[32,4,1024]{2,1,0:T(4,128)(2,1)S(1)}, u32[]{:S(2)}, u32[]{:S(2)}) collective-permute-start(bf16[32,4,1024]{2,1,0:T(4,128)(2,1)S(1)} %get-tuple-element.28), channel_id=1, source_target_pairs={{8,0},{10,2},{12,4},{14,6},{0,8},{2,10},{4,12},{6,14},{24,16},{26,... | collective-permute-start | bytes 786440 | tf_op jit(solution)/shard_map/ppermute | solution.py:346
  33.5 6.4 %collective-permute-start.3 = (bf16[32,4,1024]{2,1,0:T(4,128)(2,1)S(1)}, bf16[32,4,1024]{2,1,0:T(4,128)(2,1)S(1)}, u32[]{:S(2)}, u32[]{:S(2)}) collective-permute-start(bf16[32,4,1024]{2,1,0:T(4,128)(2,1)S(1)} %get-tuple-element.27), channel_id=1, source_target_pairs={{32,0},{34,2},{36,4},{38,6},{40,8},{42,10},{44,12},{46,14},{48,16}... | collective-permute-start | bytes 786440 | tf_op jit(solution)/shard_map/ppermute | solution.py:345
  37.6 3.0 %collective-permute-start.2 = (bf16[32,4,1024]{2,1,0:T(4,128)(2,1)S(1)}, bf16[32,4,1024]{2,1,0:T(4,128)(2,1)S(1)}, u32[]{:S(2)}, u32[]{:S(2)}) collective-permute-start(bf16[32,4,1024]{2,1,0:T(4,128)(2,1)S(1)} %collective-permute-done.1.low_ref), channel_id=1, source_target_pairs={{0,1},{2,3},{4,5},{6,7},{8,9},{10,11},{12,13},{14,15},{16,17},{18,... | collective-permute-start | bytes 786440 | tf_op jit(solution)/shard_map/ppermute | solution.py:351
  39.9 1.8 %collective-permute-start.4 = (bf16[32,4,1024]{2,1,0:T(4,128)(2,1)S(1)}, bf16[32,4,1024]{2,1,0:T(4,128)(2,1)S(1)}, u32[]{:S(2)}, u32[]{:S(2)}) collective-permute-start(bf16[32,4,1024]{2,1,0:T(4,128)(2,1)S(1)} %collective-permute-done.3.high_ref), channel_id=1, source_target_pairs={{0,1},{2,3},{4,5},{6,7},{8,9},{10,11},{12,13},{14,15},{16,17},{18,... | collective-permute-start | bytes 786440 | tf_op jit(solution)/shard_map/ppermute | solution.py:357
